TPU v7x, 256 devices: a whole 4x4x8 slice. The times are simulated.
256 devices in a mesh: blk: 16 (over x, y_lo, core), rep: 16 (over y_hi, z).
Axes of the slice: x: 4, y: 4 (y_hi: 2, y_lo: 2; y = y_hi * 2 + y_lo), z: 8, core: 2. Of those that a mesh axis runs over, the one named last changes fastest.
Arguments:
- kinematics: float32 [6, 65536], P(None, 'blk'), may hold values from -6 to 6
- derivatives: float32 [6, 65536], P(None, 'blk'), may hold values from -6 to 6
- masses: float32 [65536], P('blk'), may hold values from 0.2 to 5
- last_time: float32 [65536], P('blk'), may hold values from -0.25 to -0.0625
- block_list: int32 [2, 16, 16, 2], replicated, may hold values from 0 to 31, as said below
- block_count: int32 [2, 16, 16], replicated, may hold values from 0 to 2, as said below
Outputs:
- new_kinematics: float32 [6, 65536], P(None, 'blk')
- new_derivatives: float32 [6, 65536], P(None, 'blk')
Inputs may be any that keep to these rules, and one draw needn't show every extreme that they name: `block_list`: for each step and blk index the 32 listed block numbers are distinct. Slots at or past a device's count are ignored. `block_count`: in every step some device's count is 2.
All inputs are finite; a program needn't handle non-finite values.
Results may differ from a plain program's by a relative error of at most 0.0003.
Values sent between devices are 32-bit elements; how exact they have to be, the bound alone decides.
No kernel may reach another device: no remote copies, remote signals or barrier semaphores. Data moves between devices by JAX's collectives and lax.ppermute only.
A program may use at most 64 MiB of HBM per device.

v0:
```python
import jax
import jax.numpy as jnp
from jax import lax
from jax.sharding import PartitionSpec as P

BLOCK = 128
CAP = 2
STEPS = 2


step_length = 0.125
softening = 0.0025


def predict(kinematics, derivatives, interval):
    position = kinematics[:3]
    velocity = kinematics[3:]
    acceleration = derivatives[:3]
    jerk_old = derivatives[3:]
    new_position = position + interval * (
        velocity + interval * (acceleration * 0.5 + interval * jerk_old / 6.0)
    )
    new_velocity = velocity + interval * (acceleration + interval * jerk_old * 0.5)
    return jnp.concatenate([new_position, new_velocity], axis=0)


def pair_forces(targets, sources):
    delta_x = sources[0][None, :] - targets[0][:, None]
    delta_y = sources[1][None, :] - targets[1][:, None]
    delta_z = sources[2][None, :] - targets[2][:, None]
    delta_u = sources[3][None, :] - targets[3][:, None]
    delta_v = sources[4][None, :] - targets[4][:, None]
    delta_w = sources[5][None, :] - targets[5][:, None]
    radius_sq = delta_x * delta_x + delta_y * delta_y + delta_z * delta_z + softening
    inverse = lax.rsqrt(radius_sq)
    inverse_sq = inverse * inverse
    weight = sources[6][None, :] * inverse * inverse_sq
    radial = 3.0 * (delta_x * delta_u + delta_y * delta_v + delta_z * delta_w) * inverse_sq
    components = [
        jnp.sum(weight * delta_x, axis=1),
        jnp.sum(weight * delta_y, axis=1),
        jnp.sum(weight * delta_z, axis=1),
        jnp.sum(weight * (delta_u - radial * delta_x), axis=1),
        jnp.sum(weight * (delta_v - radial * delta_y), axis=1),
        jnp.sum(weight * (delta_w - radial * delta_z), axis=1),
    ]
    return jnp.stack(components, axis=0)


def field_forces(targets, sources, shard_width):
    pieces = sources.reshape(7, -1, shard_width).transpose(1, 0, 2)

    def add_piece(gathered_sum, incoming):
        return (gathered_sum + pair_forces(targets, incoming), None)

    initial = jnp.zeros((6, targets.shape[1]), jnp.float32)
    result, unused = lax.scan(add_piece, initial, pieces)
    return result


def correct(predicted, old_deriv, forces, interval):
    change = old_deriv[:3] - forces[:3]
    second_term = -6.0 * change - interval * (4.0 * old_deriv[3:] + 2.0 * forces[3:])
    third_term = 12.0 * change + 6.0 * interval * (old_deriv[3:] + forces[3:])
    new_position = predicted[:3] + interval * interval * (second_term / 24.0 + third_term / 120.0)
    new_velocity = predicted[3:] + interval * (second_term / 6.0 + third_term / 24.0)
    return jnp.concatenate([new_position, new_velocity], axis=0)


def assign(listed, counted):
    column_slot = jnp.arange(listed.shape[2], dtype=jnp.int32)
    is_valid = column_slot[None, None, :] < counted[:, :, None]
    picked_ids, picked_valid = (listed, is_valid)
    return (picked_ids, picked_valid)


def per_device(kinematics, derivatives, masses, last_time, block_list, block_count):
    shard_width = kinematics.shape[1]
    block_total = shard_width // BLOCK
    blk_devices = lax.axis_size("blk")
    blk_index = lax.axis_index("blk")
    rep_index = lax.axis_index("rep")
    scaled = masses / (shard_width * blk_devices)
    for step_number in range(STEPS):
        time_now = step_number * step_length
        predicted = predict(kinematics, derivatives, time_now - last_time)
        sources = jnp.concatenate([predicted, scaled[None, :]], axis=0)
        column_ids, column_valid = assign(block_list[step_number], block_count[step_number])
        local_ids = lax.dynamic_index_in_dim(column_ids, blk_index, 0, keepdims=False)
        local_valid = lax.dynamic_index_in_dim(column_valid, blk_index, 0, keepdims=False)
        mine_ids = lax.dynamic_index_in_dim(local_ids, rep_index, 0, keepdims=False)
        mine_total = jnp.sum(
            lax.dynamic_index_in_dim(local_valid, rep_index, 0, keepdims=False).astype(jnp.int32)
        )
        pred_blocks = predicted.reshape(6, block_total, BLOCK)
        mine_targets = jnp.take(pred_blocks, mine_ids, axis=1).transpose(1, 0, 2)
        zero_forces = jnp.zeros((CAP, 6, BLOCK), jnp.float32)
        incoming = lax.all_gather(sources, "blk", axis=1, tiled=True)

        def add_slot(c, totals):
            targets = lax.dynamic_index_in_dim(mine_targets, c, 0, keepdims=False)
            current = lax.dynamic_index_in_dim(totals, c, 0, keepdims=False)
            return lax.dynamic_update_index_in_dim(
                totals, current + field_forces(targets, incoming, shard_width), c, 0
            )

        forces = lax.fori_loop(0, mine_total, add_slot, zero_forces)
        column_forces = lax.all_gather(forces, "rep", axis=0, tiled=True)
        flat_ids = local_ids.reshape(-1)
        flat_valid = local_valid.reshape(-1)
        kin_blocks = kinematics.reshape(6, block_total, BLOCK)
        der_blocks = derivatives.reshape(6, block_total, BLOCK)
        last_blocks = last_time.reshape(block_total, BLOCK)
        pred_rows = jnp.take(pred_blocks, flat_ids, axis=1).transpose(1, 0, 2)
        old_deriv = jnp.take(der_blocks, flat_ids, axis=1).transpose(1, 0, 2)
        old_last = jnp.take(last_blocks, flat_ids, axis=0)
        corrected = jax.vmap(correct)(pred_rows, old_deriv, column_forces, time_now - old_last)
        stacked = jnp.concatenate([corrected, column_forces], axis=1)
        selected = (
            flat_ids[:, None] == jnp.arange(block_total, dtype=jnp.int32)[None, :]
        ) & flat_valid[:, None]
        placed = jnp.einsum(
            "sk,sfb->fkb", selected.astype(jnp.float32), stacked, precision=lax.Precision.HIGHEST
        )
        covered = jnp.any(selected, axis=0)
        kinematics = jnp.where(covered[None, :, None], placed[:6], kin_blocks).reshape(
            6, shard_width
        )
        derivatives = jnp.where(covered[None, :, None], placed[6:], der_blocks).reshape(
            6, shard_width
        )
        last_time = jnp.where(covered[:, None], time_now, last_blocks).reshape(shard_width)
    return (kinematics, derivatives)


def solution(mesh):
    return jax.shard_map(
        per_device,
        mesh=mesh,
        in_specs=(P(None, "blk"), P(None, "blk"), P("blk"), P("blk"), P(), P()),
        out_specs=(P(None, "blk"), P(None, "blk")),
        check_vma=False,
    )
```

profile of v0, /device:TPU:32, one launch (start us, length us, event | category | flops | bytes accessed | tf_op | source)
XLA Modules:
  0.0 505.8 jit_solution(14419827759653933386)
XLA Ops:
  7.2 0.0 all-gather.3.cloned.1.call-start
  7.2 0.7 slice_bitcast_fusion.17
  7.9 0.1 iota_compare_fusion
  8.0 0.7 broadcast_multiply_fusion.2
  8.8 0.7 fusion.75
  9.5 0.1 copy.42
  9.6 0.1 eq.34
  9.7 0.1 and.37
  9.8 0.1 fusion.59
  9.9 0.8 select_subtract_fusion.2
  10.7 1.2 multiply_add_fusion.1
  11.9 0.7 pad_maximum_fusion.1
  12.6 0.0 all-gather.3.cloned.1.call-update
  12.6 0.0 all-gather.5.cloned.1.call-start
  12.7 0.6 fusion.70
  13.3 0.2 fusion.67
  13.5 0.1 copy.41
  13.6 0.1 eq.30
  13.8 0.5 gather_fusion.3
  14.3 0.6 gather_fusion
  14.9 1.5 gather_fusion.2
  16.4 1.3 gather_fusion.1
  17.7 0.1 broadcast_select_fusion.2
  17.8 0.1 fusion.74
  17.9 0.1 copy_select_fusion.2
  18.0 33.9 %all-gather.3.cloned.1.call-done = f32[7,65536]{1,0:T(8,128)} async-done(((f32[7,4096]{1,0:T(8,128)}), f32[7,65536]{1,0:T(8,128)}) %all-gather.3.cloned.1.call-update) | async-done | bytes 1835024 | tf_op jit(solution)/shard_map/all_gather | solution.py:98
  51.9 0.0 copy-start.1
  51.9 0.0 copy-start.2
  51.9 0.7 while.43
  52.6 0.0 copy-start
  52.6 197.6 %all_gather.13 = f32[32,6,128]{2,1,0:T(8,128)S(1)} all-gather(f32[2,6,128]{2,1,0:T(8,128)S(1)} %get-tuple-element.105), channel_id=1, replica_groups=mesh['blk'=16,'rep'=16] {'rep'}, dimensions={0}, use_global_device_ids=true | all-gather | bytes 104448 | tf_op jit(solution)/shard_map/all_gather | solution.py:108
  250.3 0.2 convolution_bitcast_fusion.1
  250.5 0.0 copy-done.1
  250.5 0.0 copy-done.2
  250.5 0.1 bitcast_select_fusion
  250.7 0.1 fusion.50
  250.8 0.7 pad_maximum_fusion
  251.5 0.0 all-gather.5.cloned.1.call-update
  251.6 0.2 fusion.68
  251.7 0.1 iota_compare_fusion.1
  251.9 0.7 fusion.69
  252.5 0.1 and.34
  252.6 0.0 copy-done
  252.6 0.1 broadcast_select_fusion
  252.7 0.6 gather_fusion.5
  253.3 0.1 fusion.55
  253.4 0.1 fusion.73
  253.5 0.1 copy.51
  253.6 0.1 copy.49
  253.7 0.6 gather_fusion.4
  254.3 0.5 gather_fusion.7
  254.8 0.6 gather_fusion.6
  255.4 0.1 broadcast_select_fusion.1
  255.5 0.1 copy_select_fusion
  255.6 36.7 %all-gather.5.cloned.1.call-done = f32[7,65536]{1,0:T(8,128)} async-done(((f32[7,4096]{1,0:T(8,128)}), f32[7,65536]{1,0:T(8,128)}) %all-gather.5.cloned.1.call-update) | async-done | bytes 1835024 | tf_op jit(solution)/shard_map/all_gather | solution.py:98
  292.2 0.6 while.45
  292.9 204.3 %all_gather.15 = f32[32,6,128]{2,1,0:T(8,128)S(1)} all-gather(f32[2,6,128]{2,1,0:T(8,128)S(1)} %get-tuple-element.106), channel_id=1, replica_groups=mesh['blk'=16,'rep'=16] {'rep'}, dimensions={0}, use_global_device_ids=true | all-gather | bytes 104448 | tf_op jit(solution)/shard_map/all_gather | solution.py:108
  497.2 0.2 convolution_bitcast_fusion
  497.4 0.1 fusion.44
  497.5 0.7 copy.98
  498.3 0.7 copy.97
  (27 shorter events, 0.3 us)
Async XLA Ops:
  7.2 44.8 %all-gather.3.cloned.1.call-start = ((), (), s32[]{:S(2)}) async-start(), calls=%async_computation | async-start | bytes 2228224 | tf_op jit(solution)/shard_map/all_gather | solution.py:98
  12.6 279.6 %all-gather.5.cloned.1.call-start = ((), (), s32[]{:S(2)}) async-start(), calls=%async_computation.1 | async-start | bytes 2228224 | tf_op jit(solution)/shard_map/all_gather | solution.py:98
  51.9 198.6 %copy-start.1 = (f32[6,4096]{1,0:T(8,128)S(1)}, f32[6,4096]{1,0:T(8,128)}, u32[]{:S(2)}) copy-start(f32[6,4096]{1,0:T(8,128)} %param.21) | copy-start | bytes 294916
  51.9 198.6 %copy-start.2 = (f32[6,4096]{1,0:T(8,128)S(1)}, f32[6,4096]{1,0:T(8,128)}, u32[]{:S(2)}) copy-start(f32[6,4096]{1,0:T(8,128)} %param.20) | copy-start | bytes 294916
  52.6 200.0 %copy-start = (f32[4096]{0:T(1024)S(1)}, f32[4096]{0:T(1024)}, u32[]{:S(2)}) copy-start(f32[4096]{0:T(1024)} %param.23) | copy-start | bytes 49156
Sparse Core Ops, SparseCore 0:
  12.7 39.1 all-gather.2
  251.7 40.5 all-gather.4
where the time goes:
time: 510 us; the launch traced here: 506 us
  blocking collectives  402 us (79%)
  waiting for transfers between devices  70.6 us (14%)
  between operations  14.4 us (3%)
  local copies, waits for them, and re-layouts  10.2 us (2%)
  other arithmetic  6.95 us (1%)
    all_gather x2, blocking collectives, per_device(): column_forces = lax.all_gather(forces, 'rep', axis=0, tiled=True)  402 us
    all_gather x2, waiting for transfers between devices, per_device(): incoming = lax.all_gather(sources, 'blk', axis=1, tiled=True)  70.6 us
  transfers between devices with their start and end apart: 2, of which 2 were waited for; matrix products, arithmetic and copies ran while one was open for 2% of the time, Pallas kernels for 0%

commit v1 on v0

v1 whole, which is shorter than its diff:
```python
import functools

import jax
import jax.numpy as jnp
from jax import lax
from jax.experimental import pallas as pl
from jax.experimental.pallas import tpu as pltpu
from jax.sharding import PartitionSpec as P

BLOCK = 128
CAP = 2
STEPS = 2
ROWS = 8
F32 = jnp.float32
BF16 = jnp.bfloat16

step_length = 0.125
softening = 0.0025
grid_shift = 1.5 * 2.0**16
piece_rows = 128
chunk = 256
prep_width = 512


def predict(position, velocity, acceleration, jerk_old, interval):
    new_position = position + interval * (
        velocity + interval * (acceleration * 0.5 + interval * jerk_old / 6.0)
    )
    new_velocity = velocity + interval * (acceleration + interval * jerk_old * 0.5)
    return jnp.concatenate([new_position, new_velocity], axis=0)


def correct(predicted, old_deriv, forces, interval):
    change = old_deriv[:3] - forces[:3]
    second_term = -6.0 * change - interval * (4.0 * old_deriv[3:] + 2.0 * forces[3:])
    third_term = 12.0 * change + 6.0 * interval * (old_deriv[3:] + forces[3:])
    new_position = predicted[:3] + interval * interval * (second_term / 24.0 + third_term / 120.0)
    new_velocity = predicted[3:] + interval * (second_term / 6.0 + third_term / 24.0)
    return jnp.concatenate([new_position, new_velocity], axis=0)


def round_short(value):
    return value.astype(BF16).astype(F32)


def split_three(value):
    high = round_short(value)
    rest = value - high
    middle = round_short(rest)
    return high, middle, rest - middle


def stack_three(value):
    return jnp.concatenate(split_three(value), axis=0)


def star_pieces(stars):
    position, velocity = stars[0:3], stars[3:6]
    coarse = (position + grid_shift) - grid_shift
    coarse_a = round_short(coarse)
    coarse_b = coarse - coarse_a
    fine = position - coarse
    fine_a = round_short(fine)
    fine_b = round_short(fine - fine_a)
    fine = fine_a + fine_b
    square = jnp.sum(coarse * coarse, axis=0, keepdims=True)
    cross = jnp.sum(2.0 * coarse * fine + fine * fine, axis=0, keepdims=True)
    mixed = jnp.sum(position * velocity, axis=0, keepdims=True)
    return coarse_a, coarse_b, fine_a, fine_b, square, cross, mixed


def source_pieces(stars):
    ca, cb, fa, fb, square, cross, mixed = star_pieces(stars)
    va, vb, vc = split_three(stars[3:6])
    width = stars.shape[1]
    one = jnp.ones((3, width), F32)
    rows = [ca, ca, cb, cb, stack_three(square), one, jnp.zeros((6, width), F32)]
    rows += [ca, ca, cb, cb, fa, fa, fb, fb, fa, fa, stack_three(cross), one]
    rows += [va, va, va, vb, vb, vc, stack_three(mixed), one]
    rows += [jnp.zeros((piece_rows - 84, width), F32)]
    return jnp.concatenate(rows, axis=0)


def target_pieces(stars):
    ca, cb, fa, fb, square, cross, mixed = star_pieces(stars)
    va, vb, vc = split_three(stars[3:6])
    xa, xb, xc = split_three(stars[0:3])
    width = stars.shape[1]
    one = jnp.ones((3, width), F32)
    zero = jnp.zeros((3, width), F32)
    da, db = -2.0 * ca, -2.0 * cb
    ea, eb = -2.0 * fa, -2.0 * fb
    tail = jnp.zeros((piece_rows - 84, width), F32)
    radius = [da, db, da, db, one, stack_three(square), zero, zero]
    radius += [ea, eb, ea, eb, da, db, da, db, ea, eb, one, stack_three(cross + softening)]
    radius += [zero] * 8 + [tail]
    moving = [-va, -vb, -va, -vb, zero, zero, zero, zero]
    moving += [-vc, zero, zero, zero, -va, -vb, -va, zero, zero, zero, zero, zero]
    moving += [-xa, -xb, -xc, -xa, -xb, -xa, one, stack_three(mixed), tail]
    both = [jnp.concatenate(radius, axis=0), jnp.concatenate(moving, axis=0)]
    return jnp.concatenate(both, axis=1).astype(BF16)


def block_at(number):
    return pl.ds(pl.multiple_of(number * BLOCK, BLOCK), BLOCK)


def predicted_block(kin_ref, der_ref, last_ref, where, time_now):
    kin, der = kin_ref[:, where], der_ref[:, where]
    return predict(kin[:3], kin[3:], der[:3], der[3:], time_now - last_ref[:, where])


def list_place(step, blk, rep, slot, n_blk, n_rep):
    return ((step * n_blk + blk) * n_rep + rep) * CAP + slot


def write_targets(step, n_blk, n_rep, list_ref, kin_ref, der_ref, last_ref, out_ref):
    blk, rep = lax.axis_index("blk"), lax.axis_index("rep")
    rows = []
    for slot in range(CAP):
        number = list_ref[list_place(step, blk, rep, slot, n_blk, n_rep)]
        rows.append(predicted_block(kin_ref, der_ref, last_ref, block_at(number), step * step_length))
        rows.append(jnp.zeros((ROWS - 6, BLOCK), F32))
    mine = jnp.concatenate(rows, axis=0)
    for other in range(n_blk):
        out_ref[other] = mine


def targets_kernel(step, n_blk, n_rep, list_ref, kin_ref, der_ref, last_ref, out_ref):
    write_targets(step, n_blk, n_rep, list_ref, kin_ref, der_ref, last_ref, out_ref)


def forces_kernel(
    step, n_blk, n_rep, count_ref, target_ref, kin_ref, der_ref, last_ref, mass_ref,
    out_ref, pred_ref, piece_ref, moment_ref,
):
    rep = lax.axis_index("rep")
    width = kin_ref.shape[1]
    total = jnp.zeros((6, prep_width), F32)
    for part in range(width // prep_width):
        where = pl.ds(part * prep_width, prep_width)
        stars = predicted_block(kin_ref, der_ref, last_ref, where, step * step_length)
        pred_ref[:, where] = stars
        total = total + stars
    centre = jnp.sum(total, axis=1, keepdims=True) / width
    for part in range(width // prep_width):
        where = pl.ds(part * prep_width, prep_width)
        stars = pred_ref[:, where] - centre
        piece_ref[where, :] = source_pieces(stars).T.astype(BF16)
        scaled = mass_ref[:, where] / (width * n_blk)
        ones = jnp.ones((1, prep_width), F32)
        moments = jnp.concatenate([stars, ones, jnp.zeros_like(ones)], axis=0) * scaled
        moments = jnp.concatenate([stack_three(moments), jnp.zeros((8, prep_width), F32)], axis=0)
        moment_ref[:, where] = moments.astype(BF16)

    def one_slot(place, carry):
        blk = place // CAP
        slot = place % CAP
        active = slot < count_ref[(step * n_blk + blk) * n_rep + rep]

        @pl.when(active)
        def _():
            stars = target_ref[place][0:6] - centre
            against = target_pieces(stars)
            acc = jnp.zeros((32, 2 * BLOCK), F32)
            for part in range(width // chunk):
                where = pl.ds(part * chunk, chunk)
                both = jnp.dot(piece_ref[where, :], against, preferred_element_type=F32)
                inverse = lax.rsqrt(both[:, :BLOCK])
                inverse_sq = inverse * inverse
                weight = inverse * inverse_sq
                radial = weight * (inverse_sq * both[:, BLOCK:])
                pair = jnp.concatenate([weight, radial], axis=1)
                high = pair.astype(BF16)
                low = (pair - high.astype(F32)).astype(BF16)
                moments = moment_ref[:, where]
                acc = acc + jnp.dot(moments, high, preferred_element_type=F32)
                acc = acc + jnp.dot(moments, low, preferred_element_type=F32)
            acc = acc[0:8] + acc[8:16] + acc[16:24]
            by_weight, by_radial = acc[:, :BLOCK], acc[:, BLOCK:]
            sums = by_weight[0:6] - stars * by_weight[6:7]
            pull = by_radial[0:3] - stars[0:3] * by_radial[6:7]
            out_ref[place] = jnp.concatenate(
                [sums[0:3], sums[3:6] - 3.0 * pull, jnp.zeros((ROWS - 6, BLOCK), F32)], axis=0
            )

        @pl.when(jnp.logical_not(active))
        def _():
            out_ref[place] = jnp.zeros((ROWS, BLOCK), F32)

        return carry

    lax.fori_loop(0, n_blk * CAP, one_slot, 0)


def total_kernel(n_blk, n_rep, part_ref, out_ref):
    total = part_ref[0]
    for other in range(1, n_blk):
        total = total + part_ref[other]
    for other in range(n_rep):
        out_ref[other] = total


def update_kernel(
    step, n_blk, n_rep, list_ref, count_ref, force_ref, kin_ref, der_ref, last_ref,
    new_kin_ref, new_der_ref, new_last_ref, *next_refs,
):
    blk = lax.axis_index("blk")
    time_now = step * step_length
    new_kin_ref[...] = kin_ref[...]
    new_der_ref[...] = der_ref[...]
    new_last_ref[...] = last_ref[...]

    def one_slot(place, carry):
        rep = place // CAP
        slot = place % CAP

        @pl.when(slot < count_ref[(step * n_blk + blk) * n_rep + rep])
        def _():
            number = list_ref[list_place(step, blk, rep, slot, n_blk, n_rep)]
            where = block_at(number)
            predicted = predicted_block(kin_ref, der_ref, last_ref, where, time_now)
            forces = force_ref[place][0:6]
            interval = time_now - last_ref[:, where]
            new_kin_ref[:, where] = correct(predicted, der_ref[:, where], forces, interval)
            new_der_ref[:, where] = forces
            new_last_ref[:, where] = jnp.full((1, BLOCK), time_now, F32)

        return carry

    lax.fori_loop(0, n_rep * CAP, one_slot, 0)
    if next_refs:
        write_targets(
            step + 1, n_blk, n_rep, list_ref, new_kin_ref, new_der_ref, new_last_ref, next_refs[0]
        )


def shape_of(*sizes):
    return jax.ShapeDtypeStruct(sizes, F32)


def run_kernel(body, scalars, arrays, out_shape, scratch=()):
    return pl.pallas_call(
        body,
        out_shape=out_shape,
        in_specs=[pl.BlockSpec(memory_space=pltpu.SMEM)] * len(scalars)
        + [pl.BlockSpec(memory_space=pltpu.VMEM)] * len(arrays),
        out_specs=jax.tree.map(lambda leaf: pl.BlockSpec(memory_space=pltpu.VMEM), out_shape),
        scratch_shapes=list(scratch),
        compiler_params=pltpu.CompilerParams(vmem_limit_bytes=32 * 2**20),
    )(*scalars, *arrays)


def per_device(kinematics, derivatives, masses, last_time, block_list, block_count):
    width = kinematics.shape[1]
    n_blk = lax.axis_size("blk")
    n_rep = lax.axis_size("rep")
    flat_list = block_list.reshape(-1)
    flat_count = block_count.reshape(-1)
    mass = masses.reshape(1, width)
    last = last_time.reshape(1, width)
    targets = run_kernel(
        functools.partial(targets_kernel, 0, n_blk, n_rep),
        [flat_list],
        [kinematics, derivatives, last],
        shape_of(n_blk, CAP * ROWS, BLOCK),
    )
    for step in range(STEPS):
        gathered = lax.all_to_all(targets, "blk", 0, 0, tiled=True)
        partial_forces = run_kernel(
            functools.partial(forces_kernel, step, n_blk, n_rep),
            [flat_count],
            [gathered.reshape(n_blk * CAP, ROWS, BLOCK), kinematics, derivatives, last, mass],
            shape_of(n_blk * CAP, ROWS, BLOCK),
            [
                pltpu.VMEM((6, width), F32),
                pltpu.VMEM((width, piece_rows), BF16),
                pltpu.VMEM((32, width), BF16),
            ],
        )
        partial_forces = partial_forces.reshape(n_blk, CAP * ROWS, BLOCK)
        spread = lax.all_to_all(partial_forces, "blk", 0, 0, tiled=True)
        mine = run_kernel(
            functools.partial(total_kernel, n_blk, n_rep),
            [],
            [spread],
            shape_of(n_rep, CAP * ROWS, BLOCK),
        )
        forces = lax.all_to_all(mine, "rep", 0, 0, tiled=True)
        out_shape = [shape_of(6, width), shape_of(6, width), shape_of(1, width)]
        if step + 1 < STEPS:
            out_shape.append(shape_of(n_blk, CAP * ROWS, BLOCK))
        kinematics, derivatives, last, *rest = run_kernel(
            functools.partial(update_kernel, step, n_blk, n_rep),
            [flat_list, flat_count],
            [forces.reshape(n_rep * CAP, ROWS, BLOCK), kinematics, derivatives, last],
            out_shape,
        )
        if rest:
            targets = rest[0]
    return (kinematics, derivatives)


def solution(mesh):
    return jax.shard_map(
        per_device,
        mesh=mesh,
        in_specs=(P(None, "blk"), P(None, "blk"), P("blk"), P("blk"), P(), P()),
        out_specs=(P(None, "blk"), P(None, "blk")),
        check_vma=False,
    )
```

time: 510 us -> 127 us (0.25)
  blocking collectives: 402 us -> 68.4 us
  waiting for transfers between devices: 70.6 us -> 6.36 us
  Pallas kernels: 0 us -> 43.3 us
  between operations: 14.4 us -> 0.71 us
  local copies, waits for them, and re-layouts: 10.2 us -> 2.06 us
  other arithmetic: 6.95 us -> 0 us
  starting transfers between devices: 0.08 us -> 5.55 us
    all_gather x2 -> x0, blocking collectives: 402 us -> none  [per_device(): column_forces = lax.all_gather(forces, 'rep', axis=0, tiled=True)]
    all_gather x2 -> x0, waiting for transfers between devices: 70.6 us -> none  [per_device(): incoming = lax.all_gather(sources, 'blk', axis=1, tiled=True)]
    all_to_all x0 -> x5, blocking collectives: none -> 68.4 us  [the longest x2 41.2 us: per_device(): forces = lax.all_to_all(mine, 'rep', 0, 0, tiled=True)]
    pallas_call x0 -> x7, Pallas kernels: none -> 43.3 us  [run_kernel(): pl.pallas_call(body, out_shape=out_shape, in_specs=[pl.BlockSpec(memory_s...]
    all_to_all x0 -> x1, waiting for transfers between devices: none -> 6.36 us  [per_device(): gathered = lax.all_to_all(targets, 'blk', 0, 0, tiled=True)]
    gather x8 -> x0, local copies, waits for them, and re-layouts: 6.2 us -> none  [the longest x2 2.06 us: per_device(): old_deriv = jnp.take(der_blocks, flat_ids, axis=1).transpose(1, 0, 2)]
    all_to_all x0 -> x1, starting transfers between devices: none -> 5.55 us  [per_device(): gathered = lax.all_to_all(targets, 'blk', 0, 0, tiled=True)]
  transfers between devices with their start and end apart: 2 -> 1, of which waited for: 2 -> 1; matrix products, arithmetic and copies ran while one was open for 2% -> 0% of each run, Pallas kernels for 0% -> 0%
where the time goes in v1:
time: 127 us; the launch traced here: 126 us
  blocking collectives  68.4 us (54%)
  Pallas kernels  43.3 us (34%)
  waiting for transfers between devices  6.36 us (5%)
  starting transfers between devices  5.55 us (4%)
  local copies, waits for them, and re-layouts  2.06 us (2%)
    pallas_call x7, Pallas kernels, run_kernel(): pl.pallas_call(body, out_shape=out_shape, in_specs=[pl.BlockSpec(memory_s...  43.3 us
    all_to_all x2, blocking collectives, per_device(): forces = lax.all_to_all(mine, 'rep', 0, 0, tiled=True)  41.2 us
    all_to_all x2, blocking collectives, per_device(): spread = lax.all_to_all(partial_forces, 'blk', 0, 0, tiled=True)  18.1 us
    all_to_all x1, blocking collectives, per_device(): gathered = lax.all_to_all(targets, 'blk', 0, 0, tiled=True)  9.07 us
    all_to_all x1, waiting for transfers between devices, per_device(): gathered = lax.all_to_all(targets, 'blk', 0, 0, tiled=True)  6.36 us
    all_to_all x1, starting transfers between devices, per_device(): gathered = lax.all_to_all(targets, 'blk', 0, 0, tiled=True)  5.55 us
  transfers between devices with their start and end apart: 1, of which 1 were waited for; matrix products, arithmetic and copies ran while one was open for 0% of the time, Pallas kernels for 0%

profile of v1, /device:TPU:32, one launch (start us, length us, event | category | flops | bytes accessed | tf_op | source)
XLA Modules:
  0.0 126.4 jit_solution(6683980214760707904)
XLA Ops:
  0.6 0.0 copy-start.2
  0.6 1.0 copy.8
  1.7 0.0 copy-start
  1.7 0.0 copy-start.1
  1.7 0.2 reshape.34.list_ref
  1.8 0.0 copy-done.2
  1.8 0.7 copy-done
  2.6 0.1 copy-done.1
  2.6 1.3 %shard_map.77 = f32[16,16,128]{2,1,0:T(8,128)} custom-call(s32[1024]{0:T(1024)S(1)} %reshape.34.list_ref, f32[6,4096]{1,0:T(8,128)S(1)} %copy-done, f32[6,4096]{1,0:T(8,128)S(1)} %copy-done.1, f32[1,4096]{1,0:T(1,128)S(1)} %bitcast.16), custom_call_target="tpu_custom_call" | custom-call | tf_op jit(solution)/shard_map/pallas_call | solution.py:243
  3.9 0.0 copy-start.4
  3.9 5.5 %all-to-all-start = ((f32[16,16,128]{2,1,0:T(8,128)}), f32[16,16,128]{2,1,0:T(8,128)S(1)}, u32[]{:S(2)}, u32[]{:S(2)}) async-start(f32[16,16,128]{2,1,0:T(8,128)} %shard_map.77), calls=%async_computation | async-start | bytes 262144 | tf_op jit(solution)/shard_map/all_to_all | solution.py:269
  9.5 0.0 copy-done.4
  9.5 0.0 copy-start.3
  9.5 0.1 reshape.35.count_ref
  9.6 6.4 %all-to-all-done = f32[16,16,128]{2,1,0:T(8,128)S(1)} async-done(((f32[16,16,128]{2,1,0:T(8,128)}), f32[16,16,128]{2,1,0:T(8,128)S(1)}, u32[]{:S(2)}, u32[]{:S(2)}) %all-to-all-start) | async-done | bytes 131104 | tf_op jit(solution)/shard_map/all_to_all | solution.py:269
  15.9 0.0 copy-done.3
  15.9 14.9 %shard_map.78 = f32[32,8,128]{2,1,0:T(8,128)S(1)} custom-call(s32[512]{0:T(512)S(1)} %reshape.35.count_ref, f32[32,8,128]{2,1,0:T(8,128)S(1)} %bitcast.10, f32[6,4096]{1,0:T(8,128)S(1)} %copy-done, f32[6,4096]{1,0:T(8,128)S(1)} %copy-done.1, f32[1,4096]{1,0:T(1,128)S(1)} %bitcast.17, f32[1,4096]{1,0:T(1,128)S(1)} %bitcast.19), custom_call_target="tpu_custom_call" | custom-call | tf_op jit(solution)/shard_map/pallas_call | solution.py:243
  30.8 9.1 %all_to_all.30.part_ref = f32[16,16,128]{2,1,0:T(8,128)S(1)} all-to-all(f32[16,16,128]{2,1,0:T(8,128)S(1)} %bitcast.14), channel_id=1, replica_groups=mesh['blk'=16,'rep'=16] {'blk'}, dimensions={0} | all-to-all | bytes 262144 | tf_op jit(solution)/shard_map/all_to_all | solution.py:282
  39.9 28.0 %all_to_all.31 = f32[16,16,128]{2,1,0:T(8,128)S(1)} all-to-all(f32[16,16,128]{2,1,0:T(8,128)S(1)} %shard_map.79), channel_id=1, replica_groups=mesh['blk'=16,'rep'=16] {'rep'}, dimensions={0} | all-to-all | bytes 262144 | tf_op jit(solution)/shard_map/all_to_all | solution.py:289
  68.0 1.5 %shard_map.80 = (f32[6,4096]{1,0:T(8,128)S(1)}, f32[6,4096]{1,0:T(8,128)S(1)}, f32[1,4096]{1,0:T(1,128)S(1)}, f32[16,16,128]{2,1,0:T(8,128)S(1)}) custom-call(s32[1024]{0:T(1024)S(1)} %reshape.34.list_ref, s32[512]{0:T(512)S(1)} %reshape.35.count_ref, f32[32,8,128]{2,1,0:T(8,128)S(1)} %bitcast.12, f32[6,4096]{1,0:T(8,128)S(1)} %copy-done, ...), custom_call_target="tpu_custom_call" | custom-call | tf_op jit(solution)/shard_map/pallas_call | solution.py:243
  69.5 9.1 %all_to_all.32 = f32[16,16,128]{2,1,0:T(8,128)S(1)} all-to-all(f32[16,16,128]{2,1,0:T(8,128)S(1)} %get-tuple-element.8), channel_id=1, replica_groups=mesh['blk'=16,'rep'=16] {'blk'}, dimensions={0} | all-to-all | bytes 262144 | tf_op jit(solution)/shard_map/all_to_all | solution.py:269
  78.6 23.4 %shard_map.81 = f32[32,8,128]{2,1,0:T(8,128)S(1)} custom-call(s32[512]{0:T(512)S(1)} %reshape.35.count_ref, f32[32,8,128]{2,1,0:T(8,128)S(1)} %bitcast.13, f32[6,4096]{1,0:T(8,128)S(1)} %get-tuple-element.9.kin_ref, f32[6,4096]{1,0:T(8,128)S(1)} %get-tuple-element.10.der_ref, f32[1,4096]{1,0:T(1,128)S(1)} %get-tuple-element.11.last_ref, f32[1,4096]{1,0:T(1,128)S(1)} %bitcast.20), custom_call_target="tpu_custom_call" | custom-call | tf_op jit(solution)/shard_map/pallas_call | solution.py:243
  102.0 9.1 %all_to_all.33.part_ref = f32[16,16,128]{2,1,0:T(8,128)S(1)} all-to-all(f32[16,16,128]{2,1,0:T(8,128)S(1)} %bitcast.15), channel_id=1, replica_groups=mesh['blk'=16,'rep'=16] {'blk'}, dimensions={0} | all-to-all | bytes 262144 | tf_op jit(solution)/shard_map/all_to_all | solution.py:282
  111.1 13.2 %all_to_all.34 = f32[16,16,128]{2,1,0:T(8,128)S(1)} all-to-all(f32[16,16,128]{2,1,0:T(8,128)S(1)} %shard_map.82), channel_id=1, replica_groups=mesh['blk'=16,'rep'=16] {'rep'}, dimensions={0} | all-to-all | bytes 262144 | tf_op jit(solution)/shard_map/all_to_all | solution.py:289
  124.3 2.2 %shard_map.83 = (f32[6,4096]{1,0:T(8,128)}, f32[6,4096]{1,0:T(8,128)}, f32[1,4096]{1,0:T(1,128)}) custom-call(s32[1024]{0:T(1024)S(1)} %reshape.34.list_ref, s32[512]{0:T(512)S(1)} %reshape.35.count_ref, f32[32,8,128]{2,1,0:T(8,128)S(1)} %bitcast.11, f32[6,4096]{1,0:T(8,128)S(1)} %get-tuple-element.9.kin_ref, f32[6,4096]{1,0:T(8,128)S(1)} %get-tuple-element.10.der_ref, ...), custom_call_target="tpu_custom_call" | custom-call | tf_op jit(solution)/shard_map/pallas_call | solution.py:243
  (2 shorter events, 0.1 us)
Async XLA Ops:
  0.6 1.2 copy-start.2
  1.7 0.9 copy-start
  1.7 1.0 copy-start.1
  3.9 5.6 %copy-start.4 = (s32[2,16,16]{2,1,0:T(8,128)S(1)}, s32[2,16,16]{2,1,0:T(8,128)}, u32[]{:S(2)}) copy-start(s32[2,16,16]{2,1,0:T(8,128)} %param.11) | copy-start | bytes 6148
  3.9 12.0 %all-to-all-start = ((f32[16,16,128]{2,1,0:T(8,128)}), f32[16,16,128]{2,1,0:T(8,128)S(1)}, u32[]{:S(2)}, u32[]{:S(2)}) async-start(f32[16,16,128]{2,1,0:T(8,128)} %shard_map.77), calls=%async_computation | async-start | bytes 262144 | tf_op jit(solution)/shard_map/all_to_all | solution.py:269
  9.5 6.5 %copy-start.3 = (f32[4096]{0:T(1024)S(1)}, f32[4096]{0:T(1024)}, u32[]{:S(2)}) copy-start(f32[4096]{0:T(1024)} %param.8) | copy-start | bytes 49156

commit v2 on v1

--- a/solution.py
+++ b/solution.py
@@ -235,11 +235,267 @@
         )
 
 
+def lane_iota(rows):
+    return lax.broadcasted_iota(jnp.int32, (rows, BLOCK), 1)
+
+
+def active_rows(step, n_blk, n_rep, list_ref, count_ref):
+    lanes = lane_iota(n_rep)
+    diagonal = lax.broadcasted_iota(jnp.int32, (n_rep, n_rep), 0) == lax.broadcasted_iota(
+        jnp.int32, (n_rep, n_rep), 1
+    )
+    rows = []
+    for blk in range(n_blk):
+        counted = count_ref[step, pl.ds(blk, 1), :].astype(F32)
+        counted = jnp.sum(jnp.where(diagonal, counted, 0.0), axis=1, keepdims=True)
+        listed = list_ref[step, blk]
+        hit = jnp.zeros((n_rep, BLOCK), F32)
+        for slot in range(CAP):
+            same = (listed[:, slot : slot + 1] == lanes) & (counted > slot)
+            hit = jnp.where(same, 1.0, hit)
+        rows.append(jnp.max(hit, axis=0, keepdims=True))
+    return jnp.concatenate(rows, axis=0)
+
+
+def whole_sum(value):
+    return jnp.sum(jnp.sum(value, axis=1, keepdims=True), axis=0, keepdims=True)
+
+
+def share_blocks(n_blk, n_rep, list_ref, count_ref, table_ref):
+    blk, rep = lax.axis_index("blk"), lax.axis_index("rep")
+    first = active_rows(0, n_blk, n_rep, list_ref, count_ref)
+    second = active_rows(1, n_blk, n_rep, list_ref, count_ref)
+    in_both = first * second
+    kinds = [in_both, first - in_both, second - in_both]
+    earlier = lax.broadcasted_iota(jnp.int32, (BLOCK, BLOCK), 0) < lax.broadcasted_iota(
+        jnp.int32, (BLOCK, BLOCK), 1
+    )
+    earlier = jnp.where(earlier, 1.0, 0.0).astype(BF16)
+    above = lax.broadcasted_iota(jnp.int32, (n_blk, n_blk), 0) > lax.broadcasted_iota(
+        jnp.int32, (n_blk, n_blk), 1
+    )
+    above = jnp.where(above, 1.0, 0.0).astype(BF16)
+    own_row = lax.broadcasted_iota(jnp.int32, (n_blk, BLOCK), 0) == blk
+    lanes = lane_iota(1)
+    order = lanes * n_rep + rep
+    start = jnp.zeros((1, 1), F32)
+    fits = jnp.ones((1, 1), jnp.bool_)
+    own_kind, own_place, own_number, finish, owner = [], [], [], [], []
+    for kind in kinds:
+        short = kind.astype(BF16)
+        rank = jnp.dot(short, earlier, preferred_element_type=F32)
+        before = jnp.dot(above, short, preferred_element_type=F32)
+        before = jnp.sum(before, axis=1, keepdims=True) + start
+        amount = jnp.sum(kind, axis=1, keepdims=True)
+        fits = fits & (jnp.max(amount, axis=0, keepdims=True) <= n_rep)
+        ends = (before + amount).astype(jnp.int32)
+        owner.append(jnp.sum(jnp.where(ends <= order, 1, 0), axis=0, keepdims=True))
+        place = jnp.sum(jnp.where(own_row, before + rank, 0.0), axis=0, keepdims=True)
+        own_place.append(place.astype(jnp.int32))
+        own_kind.append(jnp.sum(jnp.where(own_row, kind, 0.0), axis=0, keepdims=True) > 0.5)
+        finish.append((jnp.max(before + amount, axis=0, keepdims=True)).astype(jnp.int32))
+        if len(finish) == 1:
+            start = jnp.sum(amount, axis=0, keepdims=True)
+    both_end = finish[0]
+    total = [jnp.maximum(finish[0], finish[1]), jnp.maximum(finish[0], finish[2])]
+    for one in total:
+        fits = fits & (one <= n_rep * n_rep)
+    handler = [jnp.bitwise_and(place, n_rep - 1) for place in own_place]
+    home = []
+    for step in range(STEPS):
+        code = jnp.where(own_kind[0], handler[0] * 2, -1)
+        home.append(jnp.where(own_kind[1 + step], handler[1 + step] * 2 + 1, code))
+    places = []
+    for step in range(STEPS):
+        is_both = order < both_end
+        places.append(jnp.where(is_both, owner[0] * 4, owner[1 + step] * 4 + 2 + step))
+    scalars = jnp.where(lanes == 0, jnp.where(fits, 1, 0), 0)
+    for index in range(3):
+        mine = own_kind[index] & (handler[index] == rep)
+        number = jnp.max(jnp.where(mine, lanes, -1), axis=1, keepdims=True)
+        scalars = jnp.where(lanes == 1 + index, number, scalars)
+        spot = jnp.max(jnp.where(mine, own_place[index] // n_rep, 0), axis=1, keepdims=True)
+        scalars = jnp.where(lanes == 4 + index, spot, scalars)
+    for step in range(STEPS):
+        amount = (total[step] - rep + n_rep - 1) // n_rep
+        scalars = jnp.where(lanes == 7 + step, amount, scalars)
+    amount = (both_end - rep + n_rep - 1) // n_rep
+    scalars = jnp.where(lanes == 9, amount, scalars)
+    rows = [home[0], home[1], scalars, places[0], places[1], jnp.zeros((3, BLOCK), jnp.int32)]
+    table_ref[...] = jnp.concatenate(rows, axis=0)
+
+
+def share_kernel(
+    n_blk, n_rep, list_ref, count_ref, kin_ref, der_ref, last_ref,
+    table_ref, out_ref, scalar_ref, semaphore,
+):
+    share_blocks(n_blk, n_rep, list_ref, count_ref, table_ref)
+    copy = pltpu.make_async_copy(table_ref, scalar_ref, semaphore)
+    copy.start()
+    copy.wait()
+    where = [block_at(jnp.maximum(scalar_ref[2, 1 + index], 0)) for index in range(3)]
+    gap = jnp.zeros((2, BLOCK), F32)
+    rows = [
+        predicted_block(kin_ref, der_ref, last_ref, where[0], 0.0),
+        0.0 - last_ref[:, where[0]],
+        gap[0:1],
+        der_ref[:, where[0]],
+        gap,
+        predicted_block(kin_ref, der_ref, last_ref, where[1], 0.0),
+        gap,
+        predicted_block(kin_ref, der_ref, last_ref, where[2], step_length),
+        gap,
+    ]
+    mine = jnp.concatenate(rows, axis=0)
+    for other in range(n_blk):
+        out_ref[other] = mine
+
+
+def write_pieces(n_blk, width, kin_ref, der_ref, last_ref, mass_ref, time_now, pred_ref, piece_ref, moment_ref):
+    total = jnp.zeros((6, prep_width), F32)
+    for part in range(width // prep_width):
+        where = pl.ds(part * prep_width, prep_width)
+        stars = predicted_block(kin_ref, der_ref, last_ref, where, time_now)
+        pred_ref[:, where] = stars
+        total = total + stars
+    centre = jnp.sum(total, axis=1, keepdims=True) / width
+    for part in range(width // prep_width):
+        where = pl.ds(part * prep_width, prep_width)
+        stars = pred_ref[:, where] - centre
+        piece_ref[where, :] = source_pieces(stars).T.astype(BF16)
+        scaled = mass_ref[:, where] / (width * n_blk)
+        ones = jnp.ones((1, prep_width), F32)
+        moments = jnp.concatenate([stars, ones, jnp.zeros_like(ones)], axis=0) * scaled
+        moments = jnp.concatenate([stack_three(moments), jnp.zeros((8, prep_width), F32)], axis=0)
+        moment_ref[:, where] = moments.astype(BF16)
+    return centre
+
+
+def block_forces(stars, piece_ref, moment_ref):
+    against = target_pieces(stars)
+    acc = jnp.zeros((32, 2 * BLOCK), F32)
+    for part in range(piece_ref.shape[0] // chunk):
+        where = pl.ds(part * chunk, chunk)
+        both = jnp.dot(piece_ref[where, :], against, preferred_element_type=F32)
+        inverse = lax.rsqrt(both[:, :BLOCK])
+        inverse_sq = inverse * inverse
+        weight = inverse * inverse_sq
+        radial = weight * (inverse_sq * both[:, BLOCK:])
+        pair = jnp.concatenate([weight, radial], axis=1)
+        high = pair.astype(BF16)
+        low = (pair - high.astype(F32)).astype(BF16)
+        moments = moment_ref[:, where]
+        acc = acc + jnp.dot(moments, high, preferred_element_type=F32)
+        acc = acc + jnp.dot(moments, low, preferred_element_type=F32)
+    acc = acc[0:8] + acc[8:16] + acc[16:24]
+    by_weight, by_radial = acc[:, :BLOCK], acc[:, BLOCK:]
+    sums = by_weight[0:6] - stars * by_weight[6:7]
+    pull = by_radial[0:3] - stars[0:3] * by_radial[6:7]
+    gap = jnp.zeros((ROWS - 6, BLOCK), F32)
+    return jnp.concatenate([sums[0:3], sums[3:6] - 3.0 * pull, gap], axis=0)
+
+
+def pieces_kernel(n_blk, kin_ref, der_ref, last_ref, mass_ref, piece_ref, moment_ref, centre_ref, pred_ref):
+    width = kin_ref.shape[1]
+    centre = write_pieces(
+        n_blk, width, kin_ref, der_ref, last_ref, mass_ref, 0.0, pred_ref, piece_ref, moment_ref
+    )
+    centre_ref[...] = jnp.broadcast_to(centre, (6, BLOCK))
+
+
+def first_forces_kernel(table_ref, target_ref, piece_ref, moment_ref, centre_ref, out_ref):
+    out_ref[...] = jnp.zeros_like(out_ref)
+
+    def one(index, carry):
+        stars = target_ref[table_ref[3, index]][0:6] - centre_ref[...]
+        out_ref[index] = block_forces(stars, piece_ref, moment_ref)
+        return carry
+
+    lax.fori_loop(0, table_ref[2, 7], one, 0)
+
+
+def middle_kernel(n_rep, table_ref, force_ref, target_ref, share_ref, next_ref):
+    own = jnp.concatenate([force_ref[table_ref[2, 4]], force_ref[table_ref[2, 5]]], axis=0)
+    for other in range(n_rep):
+        share_ref[other] = own
+
+    def one(index, carry):
+        place = table_ref[4, index]
+        is_both = index < table_ref[2, 9]
+
+        @pl.when(is_both)
+        def _():
+            head, deriv = target_ref[place], target_ref[place + 1][0:6]
+            forces = force_ref[index][0:6]
+            moved = correct(head[0:6], deriv, forces, head[6:7])
+            ahead = predict(moved[:3], moved[3:], forces[:3], forces[3:], step_length)
+            next_ref[index] = jnp.concatenate([ahead, head[6:8]], axis=0)
+
+        @pl.when(jnp.logical_not(is_both))
+        def _():
+            next_ref[index] = target_ref[place]
+
+        return carry
+
+    lax.fori_loop(0, table_ref[2, 8], one, 0)
+
+
+def move_shard(step, table_ref, force_ref, kin_ref, der_ref, last_ref, new_kin_ref, new_der_ref, new_last_ref):
+    time_now = step * step_length
+    new_kin_ref[...] = kin_ref[...]
+    new_der_ref[...] = der_ref[...]
+    if new_last_ref is not None:
+        new_last_ref[...] = last_ref[...]
+
+    def one(number, carry):
+        code = table_ref[step, number]
+
+        @pl.when(code >= 0)
+        def _():
+            where = block_at(number)
+            predicted = predicted_block(kin_ref, der_ref, last_ref, where, time_now)
+            forces = force_ref[code][0:6]
+            interval = time_now - last_ref[:, where]
+            new_kin_ref[:, where] = correct(predicted, der_ref[:, where], forces, interval)
+            new_der_ref[:, where] = forces
+            if new_last_ref is not None:
+                new_last_ref[:, where] = jnp.full((1, BLOCK), time_now, F32)
+
+        return carry
+
+    lax.fori_loop(0, kin_ref.shape[1] // BLOCK, one, 0)
+
+
+def second_forces_kernel(
+    n_blk, table_ref, force_ref, target_ref, kin_ref, der_ref, last_ref, mass_ref,
+    out_ref, new_kin_ref, new_der_ref, new_last_ref, pred_ref, piece_ref, moment_ref,
+):
+    width = kin_ref.shape[1]
+    move_shard(0, table_ref, force_ref, kin_ref, der_ref, last_ref, new_kin_ref, new_der_ref, new_last_ref)
+    centre = write_pieces(
+        n_blk, width, new_kin_ref, new_der_ref, new_last_ref, mass_ref, step_length,
+        pred_ref, piece_ref, moment_ref,
+    )
+    out_ref[...] = jnp.zeros_like(out_ref)
+
+    def one(index, carry):
+        stars = target_ref[index][0:6] - centre
+        place = table_ref[4, index]
+        out_ref[(place // 4) * 2 + place % 2] = block_forces(stars, piece_ref, moment_ref)
+        return carry
+
+    lax.fori_loop(0, table_ref[2, 8], one, 0)
+
+
+def last_kernel(table_ref, force_ref, kin_ref, der_ref, last_ref, new_kin_ref, new_der_ref):
+    move_shard(1, table_ref, force_ref, kin_ref, der_ref, last_ref, new_kin_ref, new_der_ref, None)
+
+
 def shape_of(*sizes):
     return jax.ShapeDtypeStruct(sizes, F32)
 
 
-def run_kernel(body, scalars, arrays, out_shape, scratch=()):
+def run_kernel(body, scalars, arrays, out_shape, scratch=(), cost=None):
     return pl.pallas_call(
         body,
         out_shape=out_shape,
@@ -247,18 +503,17 @@
         + [pl.BlockSpec(memory_space=pltpu.VMEM)] * len(arrays),
         out_specs=jax.tree.map(lambda leaf: pl.BlockSpec(memory_space=pltpu.VMEM), out_shape),
         scratch_shapes=list(scratch),
+        cost_estimate=cost,
         compiler_params=pltpu.CompilerParams(vmem_limit_bytes=32 * 2**20),
     )(*scalars, *arrays)
 
 
-def per_device(kinematics, derivatives, masses, last_time, block_list, block_count):
+def plain_steps(kinematics, derivatives, mass, last, block_list, block_count):
     width = kinematics.shape[1]
     n_blk = lax.axis_size("blk")
     n_rep = lax.axis_size("rep")
     flat_list = block_list.reshape(-1)
     flat_count = block_count.reshape(-1)
-    mass = masses.reshape(1, width)
-    last = last_time.reshape(1, width)
     targets = run_kernel(
         functools.partial(targets_kernel, 0, n_blk, n_rep),
         [flat_list],
@@ -301,6 +556,99 @@
     return (kinematics, derivatives)
 
 
+def add_over_blk(value):
+    n_blk = lax.axis_size("blk")
+
+    def from_partner(distance):
+        return lax.ppermute(value, "blk", [(i, i ^ distance) for i in range(n_blk)])
+
+    value = value + from_partner(1)
+    value = value + from_partner(2)
+    return value + ((from_partner(4) + from_partner(12)) + from_partner(8))
+
+
+def shared_steps(kinematics, derivatives, mass, last, table, gathered):
+    width = kinematics.shape[1]
+    n_blk = lax.axis_size("blk")
+    n_rep = lax.axis_size("rep")
+    piece_shapes = [
+        jax.ShapeDtypeStruct((width, piece_rows), BF16),
+        jax.ShapeDtypeStruct((32, width), BF16),
+    ]
+    piece_scratch = [pltpu.VMEM(leaf.shape, BF16) for leaf in piece_shapes]
+    stars_scratch = pltpu.VMEM((6, width), F32)
+    pieces, moments, centre = run_kernel(
+        functools.partial(pieces_kernel, n_blk),
+        [],
+        [kinematics, derivatives, last, mass],
+        piece_shapes + [shape_of(6, BLOCK)],
+        [stars_scratch],
+    )
+    partial_forces = run_kernel(
+        first_forces_kernel,
+        [table],
+        [gathered, pieces, moments, centre],
+        shape_of(n_rep, ROWS, BLOCK),
+    )
+    forces = add_over_blk(partial_forces.reshape(n_rep * ROWS, BLOCK))
+    shares, targets = run_kernel(
+        functools.partial(middle_kernel, n_rep),
+        [table],
+        [forces.reshape(n_rep, ROWS, BLOCK), gathered],
+        [shape_of(n_rep, 2 * ROWS, BLOCK), shape_of(n_rep, ROWS, BLOCK)],
+    )
+    shares = lax.all_to_all(shares, "rep", 0, 0, tiled=True)
+    partial_forces, kinematics, derivatives, last = run_kernel(
+        functools.partial(second_forces_kernel, n_blk),
+        [table],
+        [shares.reshape(n_rep * 2, ROWS, BLOCK), targets, kinematics, derivatives, last, mass],
+        [shape_of(n_blk * 2, ROWS, BLOCK), shape_of(6, width), shape_of(6, width), shape_of(1, width)],
+        [stars_scratch] + piece_scratch,
+    )
+    spread = lax.all_to_all(
+        partial_forces.reshape(n_blk, 2 * ROWS, BLOCK), "blk", 0, 0, tiled=True
+    )
+    mine = run_kernel(
+        functools.partial(total_kernel, n_blk, n_rep),
+        [],
+        [spread],
+        shape_of(n_rep, 2 * ROWS, BLOCK),
+    )
+    shares = lax.all_to_all(mine, "rep", 0, 0, tiled=True)
+    return run_kernel(
+        last_kernel,
+        [table],
+        [shares.reshape(n_rep * 2, ROWS, BLOCK), kinematics, derivatives, last],
+        [shape_of(6, width), shape_of(6, width)],
+    )
+
+
+def per_device(kinematics, derivatives, masses, last_time, block_list, block_count):
+    width = kinematics.shape[1]
+    n_blk = lax.axis_size("blk")
+    n_rep = lax.axis_size("rep")
+    mass = masses.reshape(1, width)
+    last = last_time.reshape(1, width)
+    table, targets = run_kernel(
+        functools.partial(share_kernel, n_blk, n_rep),
+        [],
+        [block_list, block_count, kinematics, derivatives, last],
+        [jax.ShapeDtypeStruct((8, BLOCK), jnp.int32), shape_of(n_blk, 4 * ROWS, BLOCK)],
+        [pltpu.SMEM((8, BLOCK), jnp.int32), pltpu.SemaphoreType.DMA],
+    )
+    gathered = lax.all_to_all(targets, "blk", 0, 0, tiled=True)
+    gathered = gathered.reshape(n_blk * 4, ROWS, BLOCK)
+    return tuple(
+        lax.cond(
+            table[2, 0] > 0,
+            lambda: tuple(shared_steps(kinematics, derivatives, mass, last, table, gathered)),
+            lambda: tuple(
+                plain_steps(kinematics, derivatives, mass, last, block_list, block_count)
+            ),
+        )
+    )
+
+
 def solution(mesh):
     return jax.shard_map(
         per_device,

time: 127 us -> 108 us (0.85); the launches traced: 126 us -> 109 us
  blocking collectives: 68.4 us -> 41.4 us
  waiting for transfers between devices: 6.36 us -> 14.8 us
  starting transfers between devices: 5.55 us -> 10 us
  Pallas kernels: 43.3 us -> 39.7 us
    all_to_all x5 -> x3, blocking collectives: 68.4 us -> 41.4 us  [the longest x1 18.8 us: shared_steps(): shares = lax.all_to_all(shares, 'rep', 0, 0, tiled=True)]
    ppermute x0 -> x5, waiting for transfers between devices: none -> 8.31 us  [from_partner(): return lax.ppermute(value, 'blk', [(i, i ^ distance) for i in range(n_blk)])]
    ppermute x0 -> x5, starting transfers between devices: none -> 4.59 us  [from_partner(): return lax.ppermute(value, 'blk', [(i, i ^ distance) for i in range(n_blk)])]
    pallas_call x7, Pallas kernels: 43.3 us -> 39.7 us  [run_kernel(): pl.pallas_call(body, out_shape=out_shape, in_specs=[pl.BlockSpec(memory_s...]
  transfers between devices with their start and end apart: 1 -> 6, of which waited for: 1 -> 6; matrix products, arithmetic and copies ran while one was open for 0% -> 0% of each run, Pallas kernels for 0% -> 0%
where the time goes in v2:
time: 108 us; the launch traced here: 109 us
  blocking collectives  41.4 us (38%)
  Pallas kernels  39.7 us (37%)
  waiting for transfers between devices  14.8 us (14%)
  starting transfers between devices  10 us (9%)
  local copies, waits for them, and re-layouts  1.62 us (2%)
  between operations  1.37 us (1%)
    pallas_call x7, Pallas kernels, run_kernel(): pl.pallas_call(body, out_shape=out_shape, in_specs=[pl.BlockSpec(memory_s...  39.7 us
    all_to_all x1, blocking collectives, shared_steps(): shares = lax.all_to_all(shares, 'rep', 0, 0, tiled=True)  18.8 us
    all_to_all x1, blocking collectives, shared_steps(): shares = lax.all_to_all(mine, 'rep', 0, 0, tiled=True)  13.4 us
    all_to_all x1, blocking collectives, shared_steps(): lax.all_to_all(partial_forces.reshape(n_blk, 2 * ROWS, BLOCK), 'blk', 0,...  9.17 us
    ppermute x5, waiting for transfers between devices, from_partner(): return lax.ppermute(value, 'blk', [(i, i ^ distance) for i in range(n_blk)])  8.31 us
    all_to_all x1, waiting for transfers between devices, per_device(): gathered = lax.all_to_all(targets, 'blk', 0, 0, tiled=True)  6.53 us
    all_to_all x1, starting transfers between devices, per_device(): gathered = lax.all_to_all(targets, 'blk', 0, 0, tiled=True)  5.43 us
    ppermute x5, starting transfers between devices, from_partner(): return lax.ppermute(value, 'blk', [(i, i ^ distance) for i in range(n_blk)])  4.59 us
  transfers between devices with their start and end apart: 6, of which 6 were waited for; matrix products, arithmetic and copies ran while one was open for 0% of the time, Pallas kernels for 0%

profile of v2, /device:TPU:32, one launch (start us, length us, event | category | flops | bytes accessed | tf_op | source)
XLA Modules:
  0.0 109.0 jit_solution(6361628872460731267)
XLA Ops:
  0.6 0.0 copy-start.1
  0.6 0.0 copy-start
  0.7 0.0 copy-start.5
  0.7 0.0 copy-start.2
  0.7 1.1 copy.9.list_ref
  1.7 0.0 copy-done.1
  1.7 0.0 copy-done
  1.8 0.0 copy-done.5
  1.8 0.0 copy-done.2
  1.8 2.1 %shard_map.77 = (s32[8,128]{1,0:T(8,128)S(1)}, f32[16,32,128]{2,1,0:T(8,128)}) custom-call(s32[2,16,16,2]{3,2,1,0:T(8,128)S(1)} %copy.9.list_ref, s32[2,16,16]{2,1,0:T(8,128)S(1)} %copy-done.5, f32[6,4096]{1,0:T(8,128)S(1)} %copy-done, f32[6,4096]{1,0:T(8,128)S(1)} %copy-done.1, f32[1,4096]{1,0:T(1,128)S(1)} %bitcast.31), custom_call_target="tpu_custom_call" | custom-call | tf_op jit(solution)/shard_map/pallas_call | solution.py:499
  3.9 0.0 copy-start.3
  3.9 0.0 copy-start.4
  3.9 5.4 %all-to-all-start.9 = ((f32[16,32,128]{2,1,0:T(8,128)}), f32[16,32,128]{2,1,0:T(8,128)S(1)}, u32[]{:S(2)}, u32[]{:S(2)}) async-start(f32[16,32,128]{2,1,0:T(8,128)} %get-tuple-element.56), calls=%async_computation.9 | async-start | bytes 524288 | tf_op jit(solution)/shard_map/all_to_all | solution.py:639
  9.4 0.5 slice.3
  10.5 6.5 %all-to-all-done.9 = f32[16,32,128]{2,1,0:T(8,128)S(1)} async-done(((f32[16,32,128]{2,1,0:T(8,128)}), f32[16,32,128]{2,1,0:T(8,128)S(1)}, u32[]{:S(2)}, u32[]{:S(2)}) %all-to-all-start.9) | async-done | bytes 262176 | tf_op jit(solution)/shard_map/all_to_all | solution.py:639
  17.1 0.0 copy-done.3
  17.1 0.0 copy-done.4
  17.1 91.9 %conditional.1 = ((f32[6,4096]{1,0:T(8,128)}, f32[6,4096]{1,0:T(8,128)})) conditional(s32[]{:T(128)} %bitcast.13, (s32[2,16,16,2]{2,3,1,0:T(2,128)S(1)}, s32[2,16,16]{2,1,0:T(8,128)S(1)}, f32[6,4096]{1,0:T(8,128)S(1)}, f32[6,4096]{1,0:T(8,128)S(1)}, f32[1,4096]{1,0:T(1,128)S(1)}, /*index=5*/f32[1,4096]{1,0:T(1,128)S(1)}) %tuple.30, ...), branch_computations={%region_0.0_spmd, %region_1.0_spmd} | conditional | flops 81920 | bytes 2818256 | solution.py:642
  17.1 0.9 branch_1_fun.6
  18.0 16.3 %branch_1_fun.7 = f32[16,8,128]{2,1,0:T(8,128)S(1)} custom-call(s32[8,128]{1,0:T(8,128)S(1)} %get-tuple-element.36.table_ref, f32[64,8,128]{2,1,0:T(8,128)S(1)} %bitcast.29, bf16[4096,128]{1,0:T(8,128)(2,1)S(1)} %get-tuple-element.42.piece_ref, bf16[32,4096]{1,0:T(8,128)(2,1)S(1)} %get-tuple-element.43.moment_ref, f32[6,128]{1,0:T(8,128)S(1)} %get-tuple-element.44.centre_ref), custom_call_target="tpu_custom_call" | custom-call | tf_op jit(solution)/shard_map/cond/branch_1_fun/pallas_call | solution.py:499
  34.2 0.2 collective-permute-start
  34.4 1.1 %collective-permute-done = f32[128,128]{1,0:T(8,128)S(1)} collective-permute-done((f32[128,128]{1,0:T(8,128)S(1)}, f32[128,128]{1,0:T(8,128)S(1)}, u32[]{:S(2)}, u32[]{:S(2)}) %collective-permute-start) | collective-permute-done | bytes 65568 | tf_op jit(solution)/shard_map/cond/branch_1_fun/ppermute | solution.py:563
  35.6 0.8 collective-permute-start.1
  36.4 3.5 %collective-permute-done.1 = f32[128,128]{1,0:T(8,128)S(1)} collective-permute-done((f32[128,128]{1,0:T(8,128)S(1)}, f32[128,128]{1,0:T(8,128)S(1)}, u32[]{:S(2)}, u32[]{:S(2)}) %collective-permute-start.1) | collective-permute-done | bytes 65568 | tf_op jit(solution)/shard_map/cond/branch_1_fun/ppermute | solution.py:563
  40.0 1.3 %collective-permute-start.4 = (f32[128,128]{1,0:T(8,128)S(1)}, f32[128,128]{1,0:T(8,128)S(1)}, u32[]{:S(2)}, u32[]{:S(2)}) collective-permute-start(f32[128,128]{1,0:T(8,128)S(1)} %add.11), channel_id=1, source_target_pairs={{0,128},{16,144},{32,160},{48,176},{64,192},{80,208},{96,224},{112... | collective-permute-start | bytes 196616 | tf_op jit(solution)/shard_map/cond/branch_1_fun/ppermute | solution.py:563
  41.3 1.6 %collective-permute-start.3 = (f32[128,128]{1,0:T(8,128)S(1)}, f32[128,128]{1,0:T(8,128)S(1)}, u32[]{:S(2)}, u32[]{:S(2)}) collective-permute-start(f32[128,128]{1,0:T(8,128)S(1)} %add.11), channel_id=1, source_target_pairs={{0,192},{16,208},{32,224},{48,240},{64,128},{80,144},{96,160},{112... | collective-permute-start | bytes 196616 | tf_op jit(solution)/shard_map/cond/branch_1_fun/ppermute | solution.py:563
  42.9 0.6 collective-permute-start.2
  43.5 3.0 %collective-permute-done.4 = f32[128,128]{1,0:T(8,128)S(1)} collective-permute-done((f32[128,128]{1,0:T(8,128)S(1)}, f32[128,128]{1,0:T(8,128)S(1)}, u32[]{:S(2)}, u32[]{:S(2)}) %collective-permute-start.4) | collective-permute-done | bytes 65568 | tf_op jit(solution)/shard_map/cond/branch_1_fun/ppermute | solution.py:563
  46.6 0.4 collective-permute-done.3
  47.0 0.2 collective-permute-done.2
  47.2 0.9 branch_1_fun.8
  48.1 18.8 %all_to_all.46 = f32[16,16,128]{2,1,0:T(8,128)S(1)} all-to-all(f32[16,16,128]{2,1,0:T(8,128)S(1)} %get-tuple-element.45), channel_id=1, replica_groups=mesh['blk'=16,'rep'=16] {'rep'}, dimensions={0} | all-to-all | bytes 262144 | tf_op jit(solution)/shard_map/cond/branch_1_fun/all_to_all | solution.py:600
  66.8 17.6 %branch_1_fun.9 = (f32[32,8,128]{2,1,0:T(8,128)S(1)}, f32[6,4096]{1,0:T(8,128)S(1)}, f32[6,4096]{1,0:T(8,128)S(1)}, f32[1,4096]{1,0:T(1,128)S(1)}) custom-call(s32[8,128]{1,0:T(8,128)S(1)} %get-tuple-element.36.table_ref, f32[32,8,128]{2,1,0:T(8,128)S(1)} %bitcast.26, f32[16,8,128]{2,1,0:T(8,128)S(1)} %get-tuple-element.46.target_ref, ...), custom_call_target="tpu_custom_call" | custom-call | tf_op jit(solution)/shard_map/cond/branch_1_fun/pallas_call | solution.py:499
  84.5 9.2 %all_to_all.47.part_ref = f32[16,16,128]{2,1,0:T(8,128)S(1)} all-to-all(f32[16,16,128]{2,1,0:T(8,128)S(1)} %bitcast.28), channel_id=1, replica_groups=mesh['blk'=16,'rep'=16] {'blk'}, dimensions={0} | all-to-all | bytes 262144 | tf_op jit(solution)/shard_map/cond/branch_1_fun/all_to_all | solution.py:608
  93.7 13.4 %all_to_all.48 = f32[16,16,128]{2,1,0:T(8,128)S(1)} all-to-all(f32[16,16,128]{2,1,0:T(8,128)S(1)} %branch_1_fun.10), channel_id=1, replica_groups=mesh['blk'=16,'rep'=16] {'rep'}, dimensions={0} | all-to-all | bytes 262144 | tf_op jit(solution)/shard_map/cond/branch_1_fun/all_to_all | solution.py:617
  107.1 1.9 %branch_1_fun.11 = (f32[6,4096]{1,0:T(8,128)}, f32[6,4096]{1,0:T(8,128)}) custom-call(s32[8,128]{1,0:T(8,128)S(1)} %get-tuple-element.36.table_ref, f32[32,8,128]{2,1,0:T(8,128)S(1)} %bitcast.21, f32[6,4096]{1,0:T(8,128)S(1)} %get-tuple-element.48.kin_ref, f32[6,4096]{1,0:T(8,128)S(1)} %get-tuple-element.49.der_ref, f32[1,4096]{1,0:T(1,128)S(1)} %get-tuple-element.50.last_ref), custom_call_target="tpu_custom_call" | custom-call | tf_op jit(solution)/shard_map/cond/branch_1_fun/pallas_call | solution.py:499
  (4 shorter events, 0.1 us)
Async XLA Ops:
  0.6 1.1 %copy-start.1 = (f32[6,4096]{1,0:T(8,128)S(1)}, f32[6,4096]{1,0:T(8,128)}, u32[]{:S(2)}) copy-start(f32[6,4096]{1,0:T(8,128)} %der_ref.1) | copy-start | bytes 294916
  0.6 1.1 %copy-start = (f32[6,4096]{1,0:T(8,128)S(1)}, f32[6,4096]{1,0:T(8,128)}, u32[]{:S(2)}) copy-start(f32[6,4096]{1,0:T(8,128)} %kin_ref.1) | copy-start | bytes 294916
  0.7 1.1 %copy-start.5 = (s32[2,16,16]{2,1,0:T(8,128)S(1)}, s32[2,16,16]{2,1,0:T(8,128)}, u32[]{:S(2)}) copy-start(s32[2,16,16]{2,1,0:T(8,128)} %count_ref.1) | copy-start | bytes 6148
  0.7 1.1 %copy-start.2 = (f32[4096]{0:T(1024)S(1)}, f32[4096]{0:T(1024)}, u32[]{:S(2)}) copy-start(f32[4096]{0:T(1024)} %param.11) | copy-start | bytes 49156
  3.9 13.2 %copy-start.3 = (f32[4096]{0:T(1024)S(1)}, f32[4096]{0:T(1024)}, u32[]{:S(2)}) copy-start(f32[4096]{0:T(1024)} %param.10) | copy-start | bytes 49156
  3.9 13.2 %copy-start.4 = (s32[2,16,16,2]{2,3,1,0:T(2,128)S(1)}, s32[2,16,16,2]{2,3,1,0:T(2,128)}, u32[]{:S(2)}) copy-start(s32[2,16,16,2]{2,3,1,0:T(2,128)} %param.12) | copy-start | bytes 12292
  3.9 13.1 %all-to-all-start.9 = ((f32[16,32,128]{2,1,0:T(8,128)}), f32[16,32,128]{2,1,0:T(8,128)S(1)}, u32[]{:S(2)}, u32[]{:S(2)}) async-start(f32[16,32,128]{2,1,0:T(8,128)} %get-tuple-element.56), calls=%async_computation.9 | async-start | bytes 524288 | tf_op jit(solution)/shard_map/all_to_all | solution.py:639
  34.2 1.3 %collective-permute-start = (f32[128,128]{1,0:T(8,128)S(1)}, f32[128,128]{1,0:T(8,128)S(1)}, u32[]{:S(2)}, u32[]{:S(2)}) collective-permute-start(f32[128,128]{1,0:T(8,128)S(1)} %bitcast.27), channel_id=1, source_target_pairs={{0,16},{16,0},{32,48},{48,32},{64,80},{80,64},{96,112},{112,96},{1... | collective-permute-start | bytes 196616 | tf_op jit(solution)/shard_map/cond/branch_1_fun/ppermute | solution.py:563
  35.6 4.4 %collective-permute-start.1 = (f32[128,128]{1,0:T(8,128)S(1)}, f32[128,128]{1,0:T(8,128)S(1)}, u32[]{:S(2)}, u32[]{:S(2)}) collective-permute-start(f32[128,128]{1,0:T(8,128)S(1)} %bitcast_add_fusion), channel_id=1, source_target_pairs={{0,32},{16,48},{32,0},{48,16},{64,96},{80,112},{96,64},{112,80},{1... | collective-permute-start | bytes 196616 | tf_op jit(solution)/shard_map/cond/branch_1_fun/ppermute | solution.py:563
  40.0 6.6 %collective-permute-start.4 = (f32[128,128]{1,0:T(8,128)S(1)}, f32[128,128]{1,0:T(8,128)S(1)}, u32[]{:S(2)}, u32[]{:S(2)}) collective-permute-start(f32[128,128]{1,0:T(8,128)S(1)} %add.11), channel_id=1, source_target_pairs={{0,128},{16,144},{32,160},{48,176},{64,192},{80,208},{96,224},{112... | collective-permute-start | bytes 196616 | tf_op jit(solution)/shard_map/cond/branch_1_fun/ppermute | solution.py:563
  41.3 5.7 %collective-permute-start.3 = (f32[128,128]{1,0:T(8,128)S(1)}, f32[128,128]{1,0:T(8,128)S(1)}, u32[]{:S(2)}, u32[]{:S(2)}) collective-permute-start(f32[128,128]{1,0:T(8,128)S(1)} %add.11), channel_id=1, source_target_pairs={{0,192},{16,208},{32,224},{48,240},{64,128},{80,144},{96,160},{112... | collective-permute-start | bytes 196616 | tf_op jit(solution)/shard_map/cond/branch_1_fun/ppermute | solution.py:563
  42.9 4.3 %collective-permute-start.2 = (f32[128,128]{1,0:T(8,128)S(1)}, f32[128,128]{1,0:T(8,128)S(1)}, u32[]{:S(2)}, u32[]{:S(2)}) collective-permute-start(f32[128,128]{1,0:T(8,128)S(1)} %add.11), channel_id=1, source_target_pairs={{0,64},{16,80},{32,96},{48,112},{64,0},{80,16},{96,32},{112,48},{1... | collective-permute-start | bytes 196616 | tf_op jit(solution)/shard_map/cond/branch_1_fun/ppermute | solution.py:563

commit v3 on v2

--- a/solution.py
+++ b/solution.py
@@ -19,7 +19,9 @@
 grid_shift = 1.5 * 2.0**16
 piece_rows = 128
 chunk = 256
+ahead_chunk = 1024
 prep_width = 512
+first_slots = 12
 
 
 def predict(position, velocity, acceleration, jerk_old, interval):
@@ -239,32 +241,34 @@
     return lax.broadcasted_iota(jnp.int32, (rows, BLOCK), 1)
 
 
-def active_rows(step, n_blk, n_rep, list_ref, count_ref):
-    lanes = lane_iota(n_rep)
-    diagonal = lax.broadcasted_iota(jnp.int32, (n_rep, n_rep), 0) == lax.broadcasted_iota(
-        jnp.int32, (n_rep, n_rep), 1
-    )
-    rows = []
-    for blk in range(n_blk):
-        counted = count_ref[step, pl.ds(blk, 1), :].astype(F32)
-        counted = jnp.sum(jnp.where(diagonal, counted, 0.0), axis=1, keepdims=True)
-        listed = list_ref[step, blk]
-        hit = jnp.zeros((n_rep, BLOCK), F32)
+def active_rows(n_blk, n_rep, list_ref, count_ref):
+    per_row = BLOCK // n_rep
+    parts = BLOCK * n_rep // BLOCK // 4
+    lanes = lane_iota(n_blk)
+    steps = []
+    for step in range(STEPS):
+        counted = count_ref[step]
+        tiled = []
         for slot in range(CAP):
-            same = (listed[:, slot : slot + 1] == lanes) & (counted > slot)
-            hit = jnp.where(same, 1.0, hit)
-        rows.append(jnp.max(hit, axis=0, keepdims=True))
-    return jnp.concatenate(rows, axis=0)
-
-
-def whole_sum(value):
-    return jnp.sum(jnp.sum(value, axis=1, keepdims=True), axis=0, keepdims=True)
+            listed = jnp.where(counted > slot, list_ref[step, :, slot, :], -1)
+            tiled.append(jnp.concatenate([listed] * per_row, axis=1))
+        hits = []
+        for part in range(parts):
+            number = lanes // n_rep + part * per_row
+            hit = (tiled[0] == number) | (tiled[1] == number)
+            hits.append(jnp.where(hit, 1.0, 0.0))
+        steps.append(jnp.concatenate(hits, axis=1))
+    hits = jnp.concatenate(steps, axis=0).astype(BF16)
+    width = parts * BLOCK
+    rows = lax.broadcasted_iota(jnp.int32, (width, BLOCK), 0) // n_rep
+    spread = jnp.where(rows == lax.broadcasted_iota(jnp.int32, (width, BLOCK), 1), 1.0, 0.0)
+    return jnp.dot(hits, spread.astype(BF16), preferred_element_type=F32)
 
 
 def share_blocks(n_blk, n_rep, list_ref, count_ref, table_ref):
     blk, rep = lax.axis_index("blk"), lax.axis_index("rep")
-    first = active_rows(0, n_blk, n_rep, list_ref, count_ref)
-    second = active_rows(1, n_blk, n_rep, list_ref, count_ref)
+    flags = active_rows(n_blk, n_rep, list_ref, count_ref)
+    first, second = flags[:n_blk], flags[n_blk:]
     in_both = first * second
     kinds = [in_both, first - in_both, second - in_both]
     earlier = lax.broadcasted_iota(jnp.int32, (BLOCK, BLOCK), 0) < lax.broadcasted_iota(
@@ -298,8 +302,7 @@
             start = jnp.sum(amount, axis=0, keepdims=True)
     both_end = finish[0]
     total = [jnp.maximum(finish[0], finish[1]), jnp.maximum(finish[0], finish[2])]
-    for one in total:
-        fits = fits & (one <= n_rep * n_rep)
+    fits = fits & (total[0] <= n_rep * first_slots) & (total[1] <= n_rep * n_rep)
     handler = [jnp.bitwise_and(place, n_rep - 1) for place in own_place]
     home = []
     for step in range(STEPS):
@@ -310,10 +313,10 @@
         is_both = order < both_end
         places.append(jnp.where(is_both, owner[0] * 4, owner[1 + step] * 4 + 2 + step))
     scalars = jnp.where(lanes == 0, jnp.where(fits, 1, 0), 0)
+    numbers = []
     for index in range(3):
         mine = own_kind[index] & (handler[index] == rep)
-        number = jnp.max(jnp.where(mine, lanes, -1), axis=1, keepdims=True)
-        scalars = jnp.where(lanes == 1 + index, number, scalars)
+        numbers.append(jnp.sum(jnp.where(mine, lanes.astype(F32), 0.0)).astype(jnp.int32))
         spot = jnp.max(jnp.where(mine, own_place[index] // n_rep, 0), axis=1, keepdims=True)
         scalars = jnp.where(lanes == 4 + index, spot, scalars)
     for step in range(STEPS):
@@ -323,17 +326,12 @@
     scalars = jnp.where(lanes == 9, amount, scalars)
     rows = [home[0], home[1], scalars, places[0], places[1], jnp.zeros((3, BLOCK), jnp.int32)]
     table_ref[...] = jnp.concatenate(rows, axis=0)
-
-
-def share_kernel(
-    n_blk, n_rep, list_ref, count_ref, kin_ref, der_ref, last_ref,
-    table_ref, out_ref, scalar_ref, semaphore,
-):
-    share_blocks(n_blk, n_rep, list_ref, count_ref, table_ref)
-    copy = pltpu.make_async_copy(table_ref, scalar_ref, semaphore)
-    copy.start()
-    copy.wait()
-    where = [block_at(jnp.maximum(scalar_ref[2, 1 + index], 0)) for index in range(3)]
+    return numbers
+
+
+def share_kernel(n_blk, n_rep, list_ref, count_ref, kin_ref, der_ref, last_ref, table_ref, out_ref):
+    numbers = share_blocks(n_blk, n_rep, list_ref, count_ref, table_ref)
+    where = [block_at(number) for number in numbers]
     gap = jnp.zeros((2, BLOCK), F32)
     rows = [
         predicted_block(kin_ref, der_ref, last_ref, where[0], 0.0),
@@ -373,22 +371,36 @@
 
 def block_forces(stars, piece_ref, moment_ref):
     against = target_pieces(stars)
-    acc = jnp.zeros((32, 2 * BLOCK), F32)
-    for part in range(piece_ref.shape[0] // chunk):
-        where = pl.ds(part * chunk, chunk)
-        both = jnp.dot(piece_ref[where, :], against, preferred_element_type=F32)
+    by_weight = jnp.zeros((32, 2 * BLOCK), F32)
+    by_radial = jnp.zeros((32, 2 * BLOCK), F32)
+    parts = piece_ref.shape[0] // ahead_chunk
+
+    def meet(part):
+        where = pl.ds(part * ahead_chunk, ahead_chunk)
+        return jnp.dot(piece_ref[where, :], against, preferred_element_type=F32)
+
+    def halves(value):
+        high = value.astype(BF16)
+        low = (value - high.astype(F32)).astype(BF16)
+        return jnp.concatenate([high, low], axis=1)
+
+    both = meet(0)
+    for part in range(parts):
+        ahead = meet(part + 1) if part + 1 < parts else None
         inverse = lax.rsqrt(both[:, :BLOCK])
         inverse_sq = inverse * inverse
         weight = inverse * inverse_sq
         radial = weight * (inverse_sq * both[:, BLOCK:])
-        pair = jnp.concatenate([weight, radial], axis=1)
-        high = pair.astype(BF16)
-        low = (pair - high.astype(F32)).astype(BF16)
-        moments = moment_ref[:, where]
-        acc = acc + jnp.dot(moments, high, preferred_element_type=F32)
-        acc = acc + jnp.dot(moments, low, preferred_element_type=F32)
-    acc = acc[0:8] + acc[8:16] + acc[16:24]
-    by_weight, by_radial = acc[:, :BLOCK], acc[:, BLOCK:]
+        moments = moment_ref[:, pl.ds(part * ahead_chunk, ahead_chunk)]
+        by_weight = by_weight + jnp.dot(moments, halves(weight), preferred_element_type=F32)
+        by_radial = by_radial + jnp.dot(moments, halves(radial), preferred_element_type=F32)
+        both = ahead
+
+    def gather_up(value):
+        value = value[0:8] + value[8:16] + value[16:24]
+        return value[:, :BLOCK] + value[:, BLOCK:]
+
+    by_weight, by_radial = gather_up(by_weight), gather_up(by_radial)
     sums = by_weight[0:6] - stars * by_weight[6:7]
     pull = by_radial[0:3] - stars[0:3] * by_radial[6:7]
     gap = jnp.zeros((ROWS - 6, BLOCK), F32)
@@ -414,8 +426,23 @@
     lax.fori_loop(0, table_ref[2, 7], one, 0)
 
 
+def flag_rows():
+    rows = lax.broadcasted_iota(jnp.int32, (CAP * ROWS, BLOCK), 0)
+    return jnp.bitwise_and(rows, ROWS - 1) == 6
+
+
+def flagged_total_kernel(n_blk, n_rep, part_ref, out_ref):
+    total = part_ref[0]
+    for other in range(1, n_blk):
+        total = total + part_ref[other]
+    total = jnp.where(flag_rows(), 1.0, total)
+    for other in range(n_rep):
+        out_ref[other] = total
+
+
 def middle_kernel(n_rep, table_ref, force_ref, target_ref, share_ref, next_ref):
     own = jnp.concatenate([force_ref[table_ref[2, 4]], force_ref[table_ref[2, 5]]], axis=0)
+    own = jnp.where(flag_rows(), 1.0, own)
     for other in range(n_rep):
         share_ref[other] = own
 
@@ -440,38 +467,41 @@
     lax.fori_loop(0, table_ref[2, 8], one, 0)
 
 
-def move_shard(step, table_ref, force_ref, kin_ref, der_ref, last_ref, new_kin_ref, new_der_ref, new_last_ref):
+def place_forces(step, table_ref, force_ref, placed_ref):
+    for number in range(placed_ref.shape[1] // BLOCK):
+        code = table_ref[step, number]
+        tile = force_ref[jnp.maximum(code, 0)]
+        tile = tile * jnp.where(code >= 0, 1.0, 0.0)
+        placed_ref[:, pl.ds(number * BLOCK, BLOCK)] = tile
+
+
+def moved_part(step, where, placed_ref, kin_ref, der_ref, last_ref):
     time_now = step * step_length
-    new_kin_ref[...] = kin_ref[...]
-    new_der_ref[...] = der_ref[...]
-    if new_last_ref is not None:
-        new_last_ref[...] = last_ref[...]
-
-    def one(number, carry):
-        code = table_ref[step, number]
-
-        @pl.when(code >= 0)
-        def _():
-            where = block_at(number)
-            predicted = predicted_block(kin_ref, der_ref, last_ref, where, time_now)
-            forces = force_ref[code][0:6]
-            interval = time_now - last_ref[:, where]
-            new_kin_ref[:, where] = correct(predicted, der_ref[:, where], forces, interval)
-            new_der_ref[:, where] = forces
-            if new_last_ref is not None:
-                new_last_ref[:, where] = jnp.full((1, BLOCK), time_now, F32)
-
-        return carry
-
-    lax.fori_loop(0, kin_ref.shape[1] // BLOCK, one, 0)
+    placed = placed_ref[:, where]
+    forces, moved = placed[0:6], placed[6:7] > 0.5
+    kin, der, last = kin_ref[:, where], der_ref[:, where], last_ref[:, where]
+    interval = time_now - last
+    predicted = predict(kin[:3], kin[3:], der[:3], der[3:], interval)
+    corrected = correct(predicted, der, forces, interval)
+    return (
+        jnp.where(moved, corrected, kin),
+        jnp.where(moved, forces, der),
+        jnp.where(moved, time_now, last),
+    )
 
 
 def second_forces_kernel(
     n_blk, table_ref, force_ref, target_ref, kin_ref, der_ref, last_ref, mass_ref,
-    out_ref, new_kin_ref, new_der_ref, new_last_ref, pred_ref, piece_ref, moment_ref,
+    out_ref, new_kin_ref, new_der_ref, new_last_ref, placed_ref, pred_ref, piece_ref, moment_ref,
 ):
     width = kin_ref.shape[1]
-    move_shard(0, table_ref, force_ref, kin_ref, der_ref, last_ref, new_kin_ref, new_der_ref, new_last_ref)
+    place_forces(0, table_ref, force_ref, placed_ref)
+    for part in range(width // prep_width):
+        where = pl.ds(part * prep_width, prep_width)
+        kin, der, last = moved_part(0, where, placed_ref, kin_ref, der_ref, last_ref)
+        new_kin_ref[:, where] = kin
+        new_der_ref[:, where] = der
+        new_last_ref[:, where] = last
     centre = write_pieces(
         n_blk, width, new_kin_ref, new_der_ref, new_last_ref, mass_ref, step_length,
         pred_ref, piece_ref, moment_ref,
@@ -487,8 +517,15 @@
     lax.fori_loop(0, table_ref[2, 8], one, 0)
 
 
-def last_kernel(table_ref, force_ref, kin_ref, der_ref, last_ref, new_kin_ref, new_der_ref):
-    move_shard(1, table_ref, force_ref, kin_ref, der_ref, last_ref, new_kin_ref, new_der_ref, None)
+def last_kernel(
+    table_ref, force_ref, kin_ref, der_ref, last_ref, new_kin_ref, new_der_ref, placed_ref
+):
+    place_forces(1, table_ref, force_ref, placed_ref)
+    for part in range(kin_ref.shape[1] // prep_width):
+        where = pl.ds(part * prep_width, prep_width)
+        kin, der, last = moved_part(1, where, placed_ref, kin_ref, der_ref, last_ref)
+        new_kin_ref[:, where] = kin
+        new_der_ref[:, where] = der
 
 
 def shape_of(*sizes):
@@ -567,34 +604,23 @@
     return value + ((from_partner(4) + from_partner(12)) + from_partner(8))
 
 
-def shared_steps(kinematics, derivatives, mass, last, table, gathered):
+def shared_steps(kinematics, derivatives, mass, last, table, gathered, pieces, moments, centre):
     width = kinematics.shape[1]
     n_blk = lax.axis_size("blk")
     n_rep = lax.axis_size("rep")
-    piece_shapes = [
-        jax.ShapeDtypeStruct((width, piece_rows), BF16),
-        jax.ShapeDtypeStruct((32, width), BF16),
-    ]
-    piece_scratch = [pltpu.VMEM(leaf.shape, BF16) for leaf in piece_shapes]
+    piece_scratch = [pltpu.VMEM((width, piece_rows), BF16), pltpu.VMEM((32, width), BF16)]
     stars_scratch = pltpu.VMEM((6, width), F32)
-    pieces, moments, centre = run_kernel(
-        functools.partial(pieces_kernel, n_blk),
-        [],
-        [kinematics, derivatives, last, mass],
-        piece_shapes + [shape_of(6, BLOCK)],
-        [stars_scratch],
-    )
     partial_forces = run_kernel(
         first_forces_kernel,
         [table],
         [gathered, pieces, moments, centre],
-        shape_of(n_rep, ROWS, BLOCK),
-    )
-    forces = add_over_blk(partial_forces.reshape(n_rep * ROWS, BLOCK))
+        shape_of(first_slots, ROWS, BLOCK),
+    )
+    forces = add_over_blk(partial_forces.reshape(first_slots * ROWS, BLOCK))
     shares, targets = run_kernel(
         functools.partial(middle_kernel, n_rep),
         [table],
-        [forces.reshape(n_rep, ROWS, BLOCK), gathered],
+        [forces.reshape(first_slots, ROWS, BLOCK), gathered],
         [shape_of(n_rep, 2 * ROWS, BLOCK), shape_of(n_rep, ROWS, BLOCK)],
     )
     shares = lax.all_to_all(shares, "rep", 0, 0, tiled=True)
@@ -603,13 +629,13 @@
         [table],
         [shares.reshape(n_rep * 2, ROWS, BLOCK), targets, kinematics, derivatives, last, mass],
         [shape_of(n_blk * 2, ROWS, BLOCK), shape_of(6, width), shape_of(6, width), shape_of(1, width)],
-        [stars_scratch] + piece_scratch,
+        [pltpu.VMEM((ROWS, width), F32), stars_scratch] + piece_scratch,
     )
     spread = lax.all_to_all(
         partial_forces.reshape(n_blk, 2 * ROWS, BLOCK), "blk", 0, 0, tiled=True
     )
     mine = run_kernel(
-        functools.partial(total_kernel, n_blk, n_rep),
+        functools.partial(flagged_total_kernel, n_blk, n_rep),
         [],
         [spread],
         shape_of(n_rep, 2 * ROWS, BLOCK),
@@ -620,6 +646,7 @@
         [table],
         [shares.reshape(n_rep * 2, ROWS, BLOCK), kinematics, derivatives, last],
         [shape_of(6, width), shape_of(6, width)],
+        [pltpu.VMEM((ROWS, width), F32)],
     )
 
 
@@ -632,16 +659,30 @@
     table, targets = run_kernel(
         functools.partial(share_kernel, n_blk, n_rep),
         [],
-        [block_list, block_count, kinematics, derivatives, last],
+        [block_list.transpose(0, 1, 3, 2), block_count, kinematics, derivatives, last],
         [jax.ShapeDtypeStruct((8, BLOCK), jnp.int32), shape_of(n_blk, 4 * ROWS, BLOCK)],
-        [pltpu.SMEM((8, BLOCK), jnp.int32), pltpu.SemaphoreType.DMA],
     )
     gathered = lax.all_to_all(targets, "blk", 0, 0, tiled=True)
     gathered = gathered.reshape(n_blk * 4, ROWS, BLOCK)
+    pieces, moments, centre = run_kernel(
+        functools.partial(pieces_kernel, n_blk),
+        [],
+        [kinematics, derivatives, last, mass],
+        [
+            jax.ShapeDtypeStruct((width, piece_rows), BF16),
+            jax.ShapeDtypeStruct((32, width), BF16),
+            shape_of(6, BLOCK),
+        ],
+        [pltpu.VMEM((6, width), F32)],
+    )
     return tuple(
         lax.cond(
             table[2, 0] > 0,
-            lambda: tuple(shared_steps(kinematics, derivatives, mass, last, table, gathered)),
+            lambda: tuple(
+                shared_steps(
+                    kinematics, derivatives, mass, last, table, gathered, pieces, moments, centre
+                )
+            ),
             lambda: tuple(
                 plain_steps(kinematics, derivatives, mass, last, block_list, block_count)
             ),

time: 108 us -> 105 us (0.972)
  Pallas kernels: 39.7 us -> 37.7 us
  waiting for transfers between devices: 14.8 us -> 13.4 us
  local copies, waits for them, and re-layouts: 1.62 us -> 0.54 us
    pallas_call x7, Pallas kernels: 39.7 us -> 37.7 us  [run_kernel(): pl.pallas_call(body, out_shape=out_shape, in_specs=[pl.BlockSpec(memory_s...]
  transfers between devices with their start and end apart: 6 -> 6, of which waited for: 6 -> 6; matrix products, arithmetic and copies ran while one was open for 0% -> 0% of each run, Pallas kernels for 0% -> 1%
where the time goes in v3:
time: 105 us
  blocking collectives  41.8 us (40%)
  Pallas kernels  37.7 us (36%)
  waiting for transfers between devices  13.4 us (13%)
  starting transfers between devices  10.1 us (10%)
  between operations  1.35 us (1%)
    pallas_call x7, Pallas kernels, run_kernel(): pl.pallas_call(body, out_shape=out_shape, in_specs=[pl.BlockSpec(memory_s...  37.7 us
    all_to_all x1, blocking collectives, shared_steps(): shares = lax.all_to_all(shares, 'rep', 0, 0, tiled=True)  18.9 us
    all_to_all x1, blocking collectives, shared_steps(): shares = lax.all_to_all(mine, 'rep', 0, 0, tiled=True)  13.6 us
    all_to_all x1, blocking collectives, shared_steps(): lax.all_to_all(partial_forces.reshape(n_blk, 2 * ROWS, BLOCK), 'blk', 0,...  9.39 us
    ppermute x5, waiting for transfers between devices, from_partner(): return lax.ppermute(value, 'blk', [(i, i ^ distance) for i in range(n_blk)])  7.76 us
    all_to_all x1, waiting for transfers between devices, per_device(): gathered = lax.all_to_all(targets, 'blk', 0, 0, tiled=True)  5.6 us
    all_to_all x1, starting transfers between devices, per_device(): gathered = lax.all_to_all(targets, 'blk', 0, 0, tiled=True)  5.56 us
    ppermute x5, starting transfers between devices, from_partner(): return lax.ppermute(value, 'blk', [(i, i ^ distance) for i in range(n_blk)])  4.59 us
  transfers between devices with their start and end apart: 6, of which 6 were waited for; matrix products, arithmetic and copies ran while one was open for 0% of the time, Pallas kernels for 1%

profile of v3, /device:TPU:32, one launch (start us, length us, event | category | flops | bytes accessed | tf_op | source)
XLA Modules:
  0.0 105.0 jit_solution(4397239955014531596)
XLA Ops:
  0.6 2.4 %shard_map.77 = (s32[8,128]{1,0:T(8,128)S(1)}, f32[16,32,128]{2,1,0:T(8,128)}) custom-call(s32[2,16,2,16]{3,2,1,0:T(2,128)} %bitcast.39, s32[2,16,16]{2,1,0:T(8,128)} %count_ref.1, f32[6,4096]{1,0:T(8,128)} %kin_ref.3, f32[6,4096]{1,0:T(8,128)} %der_ref.3, f32[1,4096]{1,0:T(1,128)} %bitcast.32), custom_call_target="tpu_custom_call" | custom-call | tf_op jit(solution)/shard_map/pallas_call | solution.py:536
  3.0 0.0 copy-start
  3.0 0.0 copy-start.1
  3.0 0.0 copy-start.2
  3.0 0.0 copy-start.3
  3.0 5.6 %all-to-all-start.9 = ((f32[16,32,128]{2,1,0:T(8,128)}), f32[16,32,128]{2,1,0:T(8,128)S(1)}, u32[]{:S(2)}, u32[]{:S(2)}) async-start(f32[16,32,128]{2,1,0:T(8,128)} %get-tuple-element.66), calls=%async_computation.9 | async-start | bytes 524288 | tf_op jit(solution)/shard_map/all_to_all | solution.py:665
  8.6 0.0 copy-done
  8.6 0.0 copy-done.1
  8.6 0.0 copy-done.2
  8.6 0.0 copy-done.3
  8.6 0.0 copy-start.4
  8.6 0.0 copy-start.5
  8.6 0.9 shard_map.78
  9.5 0.5 slice.3
  10.7 5.6 %all-to-all-done.9 = f32[16,32,128]{2,1,0:T(8,128)S(1)} async-done(((f32[16,32,128]{2,1,0:T(8,128)}), f32[16,32,128]{2,1,0:T(8,128)S(1)}, u32[]{:S(2)}, u32[]{:S(2)}) %all-to-all-start.9) | async-done | bytes 262176 | tf_op jit(solution)/shard_map/all_to_all | solution.py:665
  16.3 0.0 copy-done.4
  16.3 0.0 copy-done.5
  16.3 88.7 %conditional.1 = ((f32[6,4096]{1,0:T(8,128)}, f32[6,4096]{1,0:T(8,128)})) conditional(s32[]{:T(128)} %bitcast.14, (s32[2,16,16,2]{2,3,1,0:T(2,128)S(1)}, s32[2,16,16]{2,1,0:T(8,128)S(1)}, f32[6,4096]{1,0:T(8,128)S(1)}, f32[6,4096]{1,0:T(8,128)S(1)}, f32[1,4096]{1,0:T(1,128)S(1)}, /*index=5*/f32[1,4096]{1,0:T(1,128)S(1)}) %tuple.30, ...), branch_computations={%region_0.0_spmd, %region_1.0_spmd} | conditional | flops 61440 | bytes 2310352 | solution.py:679
  16.3 17.0 %branch_1_fun.5 = f32[12,8,128]{2,1,0:T(8,128)S(1)} custom-call(s32[8,128]{1,0:T(8,128)S(1)} %get-tuple-element.43.table_ref, f32[64,8,128]{2,1,0:T(8,128)S(1)} %bitcast.30, bf16[4096,128]{1,0:T(8,128)(2,1)S(1)} %get-tuple-element.45.piece_ref, bf16[32,4096]{1,0:T(8,128)(2,1)S(1)} %get-tuple-element.46.moment_ref, f32[6,128]{1,0:T(8,128)S(1)} %get-tuple-element.47.centre_ref), custom_call_target="tpu_custom_call" | custom-call | tf_op jit(solution)/shard_map/cond/branch_1_fun/pallas_call | solution.py:536
  33.2 0.2 collective-permute-start
  33.4 1.1 %collective-permute-done = f32[96,128]{1,0:T(8,128)S(1)} collective-permute-done((f32[96,128]{1,0:T(8,128)S(1)}, f32[96,128]{1,0:T(8,128)S(1)}, u32[]{:S(2)}, u32[]{:S(2)}) %collective-permute-start) | collective-permute-done | bytes 49184 | tf_op jit(solution)/shard_map/cond/branch_1_fun/ppermute | solution.py:600
  34.6 0.8 collective-permute-start.1
  35.4 3.4 %collective-permute-done.1 = f32[96,128]{1,0:T(8,128)S(1)} collective-permute-done((f32[96,128]{1,0:T(8,128)S(1)}, f32[96,128]{1,0:T(8,128)S(1)}, u32[]{:S(2)}, u32[]{:S(2)}) %collective-permute-start.1) | collective-permute-done | bytes 49184 | tf_op jit(solution)/shard_map/cond/branch_1_fun/ppermute | solution.py:600
  38.8 1.3 %collective-permute-start.4 = (f32[96,128]{1,0:T(8,128)S(1)}, f32[96,128]{1,0:T(8,128)S(1)}, u32[]{:S(2)}, u32[]{:S(2)}) collective-permute-start(f32[96,128]{1,0:T(8,128)S(1)} %add.11), channel_id=1, source_target_pairs={{0,128},{16,144},{32,160},{48,176},{64,192},{80,208},{96,224},{112... | collective-permute-start | bytes 147464 | tf_op jit(solution)/shard_map/cond/branch_1_fun/ppermute | solution.py:600
  40.0 1.5 %collective-permute-start.3 = (f32[96,128]{1,0:T(8,128)S(1)}, f32[96,128]{1,0:T(8,128)S(1)}, u32[]{:S(2)}, u32[]{:S(2)}) collective-permute-start(f32[96,128]{1,0:T(8,128)S(1)} %add.11), channel_id=1, source_target_pairs={{0,192},{16,208},{32,224},{48,240},{64,128},{80,144},{96,160},{112... | collective-permute-start | bytes 147464 | tf_op jit(solution)/shard_map/cond/branch_1_fun/ppermute | solution.py:600
  41.5 0.8 collective-permute-start.2
  42.3 2.7 %collective-permute-done.4 = f32[96,128]{1,0:T(8,128)S(1)} collective-permute-done((f32[96,128]{1,0:T(8,128)S(1)}, f32[96,128]{1,0:T(8,128)S(1)}, u32[]{:S(2)}, u32[]{:S(2)}) %collective-permute-start.4) | collective-permute-done | bytes 49184 | tf_op jit(solution)/shard_map/cond/branch_1_fun/ppermute | solution.py:600
  45.0 0.4 collective-permute-done.3
  45.4 0.2 collective-permute-done.2
  45.6 0.8 branch_1_fun.6
  46.5 18.9 %all_to_all.46 = f32[16,16,128]{2,1,0:T(8,128)S(1)} all-to-all(f32[16,16,128]{2,1,0:T(8,128)S(1)} %get-tuple-element.48), channel_id=1, replica_groups=mesh['blk'=16,'rep'=16] {'rep'}, dimensions={0} | all-to-all | bytes 262144 | tf_op jit(solution)/shard_map/cond/branch_1_fun/all_to_all | solution.py:626
  65.3 15.1 %branch_1_fun.7 = (f32[32,8,128]{2,1,0:T(8,128)S(1)}, f32[6,4096]{1,0:T(8,128)S(1)}, f32[6,4096]{1,0:T(8,128)S(1)}, f32[1,4096]{1,0:T(1,128)S(1)}) custom-call(s32[8,128]{1,0:T(8,128)S(1)} %get-tuple-element.43.table_ref, f32[32,8,128]{2,1,0:T(8,128)S(1)} %bitcast.27, f32[16,8,128]{2,1,0:T(8,128)S(1)} %get-tuple-element.49.target_ref, ...), custom_call_target="tpu_custom_call" | custom-call | tf_op jit(solution)/shard_map/cond/branch_1_fun/pallas_call | solution.py:536
  80.5 9.4 %all_to_all.47.part_ref = f32[16,16,128]{2,1,0:T(8,128)S(1)} all-to-all(f32[16,16,128]{2,1,0:T(8,128)S(1)} %bitcast.29), channel_id=1, replica_groups=mesh['blk'=16,'rep'=16] {'blk'}, dimensions={0} | all-to-all | bytes 262144 | tf_op jit(solution)/shard_map/cond/branch_1_fun/all_to_all | solution.py:634
  89.9 13.6 %all_to_all.48 = f32[16,16,128]{2,1,0:T(8,128)S(1)} all-to-all(f32[16,16,128]{2,1,0:T(8,128)S(1)} %branch_1_fun.8), channel_id=1, replica_groups=mesh['blk'=16,'rep'=16] {'rep'}, dimensions={0} | all-to-all | bytes 262144 | tf_op jit(solution)/shard_map/cond/branch_1_fun/all_to_all | solution.py:643
  103.5 1.5 %branch_1_fun.9 = (f32[6,4096]{1,0:T(8,128)}, f32[6,4096]{1,0:T(8,128)}) custom-call(s32[8,128]{1,0:T(8,128)S(1)} %get-tuple-element.43.table_ref, f32[32,8,128]{2,1,0:T(8,128)S(1)} %bitcast.22, f32[6,4096]{1,0:T(8,128)S(1)} %get-tuple-element.55.kin_ref, f32[6,4096]{1,0:T(8,128)S(1)} %get-tuple-element.56.der_ref, f32[1,4096]{1,0:T(1,128)S(1)} %get-tuple-element.57.last_ref), custom_call_target="tpu_custom_call" | custom-call | tf_op jit(solution)/shard_map/cond/branch_1_fun/pallas_call | solution.py:536
  (4 shorter events, 0.1 us)
Async XLA Ops:
  3.0 5.6 %copy-start = (f32[6,4096]{1,0:T(8,128)S(1)}, f32[6,4096]{1,0:T(8,128)}, u32[]{:S(2)}) copy-start(f32[6,4096]{1,0:T(8,128)} %kin_ref.3) | copy-start | bytes 294916
  3.0 5.6 %copy-start.1 = (f32[6,4096]{1,0:T(8,128)S(1)}, f32[6,4096]{1,0:T(8,128)}, u32[]{:S(2)}) copy-start(f32[6,4096]{1,0:T(8,128)} %der_ref.3) | copy-start | bytes 294916
  3.0 5.6 %copy-start.2 = (f32[4096]{0:T(1024)S(1)}, f32[4096]{0:T(1024)}, u32[]{:S(2)}) copy-start(f32[4096]{0:T(1024)} %param.11) | copy-start | bytes 49156
  3.0 5.6 %copy-start.3 = (f32[4096]{0:T(1024)S(1)}, f32[4096]{0:T(1024)}, u32[]{:S(2)}) copy-start(f32[4096]{0:T(1024)} %param.10) | copy-start | bytes 49156
  3.0 13.3 %all-to-all-start.9 = ((f32[16,32,128]{2,1,0:T(8,128)}), f32[16,32,128]{2,1,0:T(8,128)S(1)}, u32[]{:S(2)}, u32[]{:S(2)}) async-start(f32[16,32,128]{2,1,0:T(8,128)} %get-tuple-element.66), calls=%async_computation.9 | async-start | bytes 524288 | tf_op jit(solution)/shard_map/all_to_all | solution.py:665
  8.6 7.7 %copy-start.4 = (s32[2,16,16,2]{2,3,1,0:T(2,128)S(1)}, s32[2,16,16,2]{2,3,1,0:T(2,128)}, u32[]{:S(2)}) copy-start(s32[2,16,16,2]{2,3,1,0:T(2,128)} %param.12) | copy-start | bytes 12292
  8.6 7.7 %copy-start.5 = (s32[2,16,16]{2,1,0:T(8,128)S(1)}, s32[2,16,16]{2,1,0:T(8,128)}, u32[]{:S(2)}) copy-start(s32[2,16,16]{2,1,0:T(8,128)} %count_ref.1) | copy-start | bytes 6148
  33.2 1.3 %collective-permute-start = (f32[96,128]{1,0:T(8,128)S(1)}, f32[96,128]{1,0:T(8,128)S(1)}, u32[]{:S(2)}, u32[]{:S(2)}) collective-permute-start(f32[96,128]{1,0:T(8,128)S(1)} %bitcast.28), channel_id=1, source_target_pairs={{0,16},{16,0},{32,48},{48,32},{64,80},{80,64},{96,112},{112,96},{1... | collective-permute-start | bytes 147464 | tf_op jit(solution)/shard_map/cond/branch_1_fun/ppermute | solution.py:600
  34.6 4.2 %collective-permute-start.1 = (f32[96,128]{1,0:T(8,128)S(1)}, f32[96,128]{1,0:T(8,128)S(1)}, u32[]{:S(2)}, u32[]{:S(2)}) collective-permute-start(f32[96,128]{1,0:T(8,128)S(1)} %bitcast_add_fusion), channel_id=1, source_target_pairs={{0,32},{16,48},{32,0},{48,16},{64,96},{80,112},{96,64},{112,80},{1... | collective-permute-start | bytes 147464 | tf_op jit(solution)/shard_map/cond/branch_1_fun/ppermute | solution.py:600
  38.8 6.3 %collective-permute-start.4 = (f32[96,128]{1,0:T(8,128)S(1)}, f32[96,128]{1,0:T(8,128)S(1)}, u32[]{:S(2)}, u32[]{:S(2)}) collective-permute-start(f32[96,128]{1,0:T(8,128)S(1)} %add.11), channel_id=1, source_target_pairs={{0,128},{16,144},{32,160},{48,176},{64,192},{80,208},{96,224},{112... | collective-permute-start | bytes 147464 | tf_op jit(solution)/shard_map/cond/branch_1_fun/ppermute | solution.py:600
  40.0 5.4 %collective-permute-start.3 = (f32[96,128]{1,0:T(8,128)S(1)}, f32[96,128]{1,0:T(8,128)S(1)}, u32[]{:S(2)}, u32[]{:S(2)}) collective-permute-start(f32[96,128]{1,0:T(8,128)S(1)} %add.11), channel_id=1, source_target_pairs={{0,192},{16,208},{32,224},{48,240},{64,128},{80,144},{96,160},{112... | collective-permute-start | bytes 147464 | tf_op jit(solution)/shard_map/cond/branch_1_fun/ppermute | solution.py:600
  41.5 4.1 %collective-permute-start.2 = (f32[96,128]{1,0:T(8,128)S(1)}, f32[96,128]{1,0:T(8,128)S(1)}, u32[]{:S(2)}, u32[]{:S(2)}) collective-permute-start(f32[96,128]{1,0:T(8,128)S(1)} %add.11), channel_id=1, source_target_pairs={{0,64},{16,80},{32,96},{48,112},{64,0},{80,16},{96,32},{112,48},{1... | collective-permute-start | bytes 147464 | tf_op jit(solution)/shard_map/cond/branch_1_fun/ppermute | solution.py:600

commit v4 on v3

--- a/solution.py
+++ b/solution.py
@@ -369,42 +369,66 @@
     return centre
 
 
-def block_forces(stars, piece_ref, moment_ref):
-    against = target_pieces(stars)
-    by_weight = jnp.zeros((32, 2 * BLOCK), F32)
-    by_radial = jnp.zeros((32, 2 * BLOCK), F32)
+def block_forces(blocks, piece_ref, moment_ref):
+    against = [target_pieces(stars) for stars in blocks]
     parts = piece_ref.shape[0] // ahead_chunk
-
-    def meet(part):
+    order = [(index, part) for index in range(len(blocks)) for part in range(parts)]
+    by_weight = [jnp.zeros((32, 2 * BLOCK), F32) for stars in blocks]
+    by_radial = [jnp.zeros((32, 2 * BLOCK), F32) for stars in blocks]
+
+    def meet(index, part):
         where = pl.ds(part * ahead_chunk, ahead_chunk)
-        return jnp.dot(piece_ref[where, :], against, preferred_element_type=F32)
+        return jnp.dot(piece_ref[where, :], against[index], preferred_element_type=F32)
 
     def halves(value):
         high = value.astype(BF16)
         low = (value - high.astype(F32)).astype(BF16)
         return jnp.concatenate([high, low], axis=1)
 
-    both = meet(0)
-    for part in range(parts):
-        ahead = meet(part + 1) if part + 1 < parts else None
+    both = meet(*order[0])
+    for turn, (index, part) in enumerate(order):
+        ahead = meet(*order[turn + 1]) if turn + 1 < len(order) else None
         inverse = lax.rsqrt(both[:, :BLOCK])
         inverse_sq = inverse * inverse
         weight = inverse * inverse_sq
         radial = weight * (inverse_sq * both[:, BLOCK:])
         moments = moment_ref[:, pl.ds(part * ahead_chunk, ahead_chunk)]
-        by_weight = by_weight + jnp.dot(moments, halves(weight), preferred_element_type=F32)
-        by_radial = by_radial + jnp.dot(moments, halves(radial), preferred_element_type=F32)
+        by_weight[index] += jnp.dot(moments, halves(weight), preferred_element_type=F32)
+        by_radial[index] += jnp.dot(moments, halves(radial), preferred_element_type=F32)
         both = ahead
 
     def gather_up(value):
         value = value[0:8] + value[8:16] + value[16:24]
         return value[:, :BLOCK] + value[:, BLOCK:]
 
-    by_weight, by_radial = gather_up(by_weight), gather_up(by_radial)
-    sums = by_weight[0:6] - stars * by_weight[6:7]
-    pull = by_radial[0:3] - stars[0:3] * by_radial[6:7]
-    gap = jnp.zeros((ROWS - 6, BLOCK), F32)
-    return jnp.concatenate([sums[0:3], sums[3:6] - 3.0 * pull, gap], axis=0)
+    results = []
+    for index, stars in enumerate(blocks):
+        on_weight, on_radial = gather_up(by_weight[index]), gather_up(by_radial[index])
+        sums = on_weight[0:6] - stars * on_weight[6:7]
+        pull = on_radial[0:3] - stars[0:3] * on_radial[6:7]
+        gap = jnp.zeros((ROWS - 6, BLOCK), F32)
+        results.append(jnp.concatenate([sums[0:3], sums[3:6] - 3.0 * pull, gap], axis=0))
+    return results
+
+
+def all_forces(amount, stars_of, store, piece_ref, moment_ref):
+    def some(first, size):
+        blocks = [stars_of(first + index) for index in range(size)]
+        results = block_forces(blocks, piece_ref, moment_ref)
+        for index, result in enumerate(results):
+            store(first + index, result)
+
+    pairs = amount // 2
+
+    def two(pair, carry):
+        some(pair * 2, 2)
+        return carry
+
+    lax.fori_loop(0, pairs, two, 0)
+
+    @pl.when(amount > pairs * 2)
+    def _():
+        some(pairs * 2, 1)
 
 
 def pieces_kernel(n_blk, kin_ref, der_ref, last_ref, mass_ref, piece_ref, moment_ref, centre_ref, pred_ref):
@@ -418,12 +442,13 @@
 def first_forces_kernel(table_ref, target_ref, piece_ref, moment_ref, centre_ref, out_ref):
     out_ref[...] = jnp.zeros_like(out_ref)
 
-    def one(index, carry):
-        stars = target_ref[table_ref[3, index]][0:6] - centre_ref[...]
-        out_ref[index] = block_forces(stars, piece_ref, moment_ref)
-        return carry
-
-    lax.fori_loop(0, table_ref[2, 7], one, 0)
+    def stars_of(index):
+        return target_ref[table_ref[3, index]][0:6] - centre_ref[...]
+
+    def store(index, result):
+        out_ref[index] = result
+
+    all_forces(table_ref[2, 7], stars_of, store, piece_ref, moment_ref)
 
 
 def flag_rows():
@@ -440,7 +465,10 @@
         out_ref[other] = total
 
 
-def middle_kernel(n_rep, table_ref, force_ref, target_ref, share_ref, next_ref):
+def middle_kernel(
+    n_rep, table_ref, term_a, term_b, term_c, term_d, target_ref, share_ref, next_ref, force_ref
+):
+    force_ref[...] = term_a[...] + ((term_b[...] + term_c[...]) + term_d[...])
     own = jnp.concatenate([force_ref[table_ref[2, 4]], force_ref[table_ref[2, 5]]], axis=0)
     own = jnp.where(flag_rows(), 1.0, own)
     for other in range(n_rep):
@@ -508,13 +536,14 @@
     )
     out_ref[...] = jnp.zeros_like(out_ref)
 
-    def one(index, carry):
-        stars = target_ref[index][0:6] - centre
+    def stars_of(index):
+        return target_ref[index][0:6] - centre
+
+    def store(index, result):
         place = table_ref[4, index]
-        out_ref[(place // 4) * 2 + place % 2] = block_forces(stars, piece_ref, moment_ref)
-        return carry
-
-    lax.fori_loop(0, table_ref[2, 8], one, 0)
+        out_ref[(place // 4) * 2 + place % 2] = result
+
+    all_forces(table_ref[2, 8], stars_of, store, piece_ref, moment_ref)
 
 
 def last_kernel(
@@ -601,7 +630,7 @@
 
     value = value + from_partner(1)
     value = value + from_partner(2)
-    return value + ((from_partner(4) + from_partner(12)) + from_partner(8))
+    return [value, from_partner(4), from_partner(12), from_partner(8)]
 
 
 def shared_steps(kinematics, derivatives, mass, last, table, gathered, pieces, moments, centre):
@@ -616,12 +645,14 @@
         [gathered, pieces, moments, centre],
         shape_of(first_slots, ROWS, BLOCK),
     )
-    forces = add_over_blk(partial_forces.reshape(first_slots * ROWS, BLOCK))
+    terms = add_over_blk(partial_forces.reshape(first_slots * ROWS, BLOCK))
+    terms = [term.reshape(first_slots, ROWS, BLOCK) for term in terms]
     shares, targets = run_kernel(
         functools.partial(middle_kernel, n_rep),
         [table],
-        [forces.reshape(first_slots, ROWS, BLOCK), gathered],
+        [*terms, gathered],
         [shape_of(n_rep, 2 * ROWS, BLOCK), shape_of(n_rep, ROWS, BLOCK)],
+        [pltpu.VMEM((first_slots, ROWS, BLOCK), F32)],
     )
     shares = lax.all_to_all(shares, "rep", 0, 0, tiled=True)
     partial_forces, kinematics, derivatives, last = run_kernel(

time: 105 us -> 102 us (0.971); the launches traced: 105 us -> 104 us
  Pallas kernels: 37.7 us -> 35 us
  blocking collectives: 41.8 us -> 43.2 us
    pallas_call x7, Pallas kernels: 37.7 us -> 35 us  [run_kernel(): pl.pallas_call(body, out_shape=out_shape, in_specs=[pl.BlockSpec(memory_s...]
    all_to_all x1, blocking collectives: 18.9 us -> 20.2 us  [shared_steps(): shares = lax.all_to_all(shares, 'rep', 0, 0, tiled=True)]
where the time goes in v4:
time: 102 us; the launch traced here: 104 us
  blocking collectives  43.2 us (42%)
  Pallas kernels  35 us (34%)
  waiting for transfers between devices  13.4 us (13%)
  starting transfers between devices  10.3 us (10%)
  between operations  1.35 us (1%)
    pallas_call x7, Pallas kernels, run_kernel(): pl.pallas_call(body, out_shape=out_shape, in_specs=[pl.BlockSpec(memory_s...  35 us
    all_to_all x1, blocking collectives, shared_steps(): shares = lax.all_to_all(shares, 'rep', 0, 0, tiled=True)  20.2 us
    all_to_all x1, blocking collectives, shared_steps(): shares = lax.all_to_all(mine, 'rep', 0, 0, tiled=True)  13.6 us
    all_to_all x1, blocking collectives, shared_steps(): lax.all_to_all(partial_forces.reshape(n_blk, 2 * ROWS, BLOCK), 'blk', 0,...  9.39 us
    ppermute x5, waiting for transfers between devices, from_partner(): return lax.ppermute(value, 'blk', [(i, i ^ distance) for i in range(n_blk)])  7.77 us
    all_to_all x1, waiting for transfers between devices, per_device(): gathered = lax.all_to_all(targets, 'blk', 0, 0, tiled=True)  5.6 us
    all_to_all x1, starting transfers between devices, per_device(): gathered = lax.all_to_all(targets, 'blk', 0, 0, tiled=True)  5.56 us
    ppermute x5, starting transfers between devices, from_partner(): return lax.ppermute(value, 'blk', [(i, i ^ distance) for i in range(n_blk)])  4.76 us
  transfers between devices with their start and end apart: 6, of which 6 were waited for; matrix products, arithmetic and copies ran while one was open for 0% of the time, Pallas kernels for 1%

profile of v4, /device:TPU:32, one launch (start us, length us, event | category | flops | bytes accessed | tf_op | source)
XLA Modules:
  0.0 103.8 jit_solution(12968958404331595184)
XLA Ops:
  0.6 2.4 %shard_map.77 = (s32[8,128]{1,0:T(8,128)S(1)}, f32[16,32,128]{2,1,0:T(8,128)}) custom-call(s32[2,16,2,16]{3,2,1,0:T(2,128)} %bitcast.45, s32[2,16,16]{2,1,0:T(8,128)} %count_ref.1, f32[6,4096]{1,0:T(8,128)} %kin_ref.3, f32[6,4096]{1,0:T(8,128)} %der_ref.3, f32[1,4096]{1,0:T(1,128)} %bitcast.38), custom_call_target="tpu_custom_call" | custom-call | tf_op jit(solution)/shard_map/pallas_call | solution.py:565
  3.0 0.0 copy-start
  3.0 0.0 copy-start.1
  3.0 0.0 copy-start.2
  3.0 0.0 copy-start.3
  3.0 5.6 %all-to-all-start.9 = ((f32[16,32,128]{2,1,0:T(8,128)}), f32[16,32,128]{2,1,0:T(8,128)S(1)}, u32[]{:S(2)}, u32[]{:S(2)}) async-start(f32[16,32,128]{2,1,0:T(8,128)} %get-tuple-element.66), calls=%async_computation.9 | async-start | bytes 524288 | tf_op jit(solution)/shard_map/all_to_all | solution.py:696
  8.6 0.0 copy-done
  8.6 0.0 copy-done.1
  8.6 0.0 copy-done.2
  8.6 0.0 copy-done.3
  8.6 0.0 copy-start.4
  8.6 0.0 copy-start.5
  8.6 0.9 shard_map.78
  9.5 0.5 slice.3
  10.7 5.6 %all-to-all-done.9 = f32[16,32,128]{2,1,0:T(8,128)S(1)} async-done(((f32[16,32,128]{2,1,0:T(8,128)}), f32[16,32,128]{2,1,0:T(8,128)S(1)}, u32[]{:S(2)}, u32[]{:S(2)}) %all-to-all-start.9) | async-done | bytes 262176 | tf_op jit(solution)/shard_map/all_to_all | solution.py:696
  16.3 0.0 copy-done.4
  16.3 0.0 copy-done.5
  16.3 87.6 %conditional.1 = ((f32[6,4096]{1,0:T(8,128)}, f32[6,4096]{1,0:T(8,128)})) conditional(s32[]{:T(128)} %bitcast.17, (s32[2,16,16,2]{2,3,1,0:T(2,128)S(1)}, s32[2,16,16]{2,1,0:T(8,128)S(1)}, f32[6,4096]{1,0:T(8,128)S(1)}, f32[6,4096]{1,0:T(8,128)S(1)}, f32[1,4096]{1,0:T(1,128)S(1)}, /*index=5*/f32[1,4096]{1,0:T(1,128)S(1)}) %tuple.30, ...), branch_computations={%region_0.0_spmd, %region_1.0_spmd} | conditional | flops 24576 | bytes 2064592 | solution.py:710
  16.3 15.5 %branch_1_fun.5 = f32[12,8,128]{2,1,0:T(8,128)S(1)} custom-call(s32[8,128]{1,0:T(8,128)S(1)} %get-tuple-element.43.table_ref, f32[64,8,128]{2,1,0:T(8,128)S(1)} %bitcast.36, bf16[4096,128]{1,0:T(8,128)(2,1)S(1)} %get-tuple-element.45.piece_ref, bf16[32,4096]{1,0:T(8,128)(2,1)S(1)} %get-tuple-element.46.moment_ref, f32[6,128]{1,0:T(8,128)S(1)} %get-tuple-element.47.centre_ref), custom_call_target="tpu_custom_call" | custom-call | tf_op jit(solution)/shard_map/cond/branch_1_fun/pallas_call | solution.py:565
  31.8 0.2 collective-permute-start
  32.0 1.1 %collective-permute-done = f32[96,128]{1,0:T(8,128)S(1)} collective-permute-done((f32[96,128]{1,0:T(8,128)S(1)}, f32[96,128]{1,0:T(8,128)S(1)}, u32[]{:S(2)}, u32[]{:S(2)}) %collective-permute-start) | collective-permute-done | bytes 49184 | tf_op jit(solution)/shard_map/cond/branch_1_fun/ppermute | solution.py:629
  33.1 1.0 collective-permute-start.1
  34.1 3.4 %collective-permute-done.1 = f32[96,128]{1,0:T(8,128)S(1)} collective-permute-done((f32[96,128]{1,0:T(8,128)S(1)}, f32[96,128]{1,0:T(8,128)S(1)}, u32[]{:S(2)}, u32[]{:S(2)}) %collective-permute-start.1) | collective-permute-done | bytes 49184 | tf_op jit(solution)/shard_map/cond/branch_1_fun/ppermute | solution.py:629
  37.5 1.3 %collective-permute-start.4 = (f32[96,128]{1,0:T(8,128)S(1)}, f32[96,128]{1,0:T(8,128)S(1)}, u32[]{:S(2)}, u32[]{:S(2)}) collective-permute-start(f32[96,128]{1,0:T(8,128)S(1)} %add.5), channel_id=1, source_target_pairs={{0,128},{16,144},{32,160},{48,176},{64,192},{80,208},{96,224},{112... | collective-permute-start | bytes 147464 | tf_op jit(solution)/shard_map/cond/branch_1_fun/ppermute | solution.py:629
  38.8 1.5 %collective-permute-start.3 = (f32[96,128]{1,0:T(8,128)S(1)}, f32[96,128]{1,0:T(8,128)S(1)}, u32[]{:S(2)}, u32[]{:S(2)}) collective-permute-start(f32[96,128]{1,0:T(8,128)S(1)} %add.5), channel_id=1, source_target_pairs={{0,192},{16,208},{32,224},{48,240},{64,128},{80,144},{96,160},{112... | collective-permute-start | bytes 147464 | tf_op jit(solution)/shard_map/cond/branch_1_fun/ppermute | solution.py:629
  40.3 0.8 collective-permute-start.2
  41.0 2.7 %collective-permute-done.4 = f32[96,128]{1,0:T(8,128)S(1)} collective-permute-done((f32[96,128]{1,0:T(8,128)S(1)}, f32[96,128]{1,0:T(8,128)S(1)}, u32[]{:S(2)}, u32[]{:S(2)}) %collective-permute-start.4) | collective-permute-done | bytes 49184 | tf_op jit(solution)/shard_map/cond/branch_1_fun/ppermute | solution.py:629
  43.7 0.4 collective-permute-done.3
  44.1 0.2 collective-permute-done.2
  44.3 0.9 branch_1_fun.6
  45.2 20.2 %all_to_all.46 = f32[16,16,128]{2,1,0:T(8,128)S(1)} all-to-all(f32[16,16,128]{2,1,0:T(8,128)S(1)} %get-tuple-element.48), channel_id=1, replica_groups=mesh['blk'=16,'rep'=16] {'rep'}, dimensions={0} | all-to-all | bytes 262144 | tf_op jit(solution)/shard_map/cond/branch_1_fun/all_to_all | solution.py:657
  65.4 13.8 %branch_1_fun.7 = (f32[32,8,128]{2,1,0:T(8,128)S(1)}, f32[6,4096]{1,0:T(8,128)S(1)}, f32[6,4096]{1,0:T(8,128)S(1)}, f32[1,4096]{1,0:T(1,128)S(1)}) custom-call(s32[8,128]{1,0:T(8,128)S(1)} %get-tuple-element.43.table_ref, f32[32,8,128]{2,1,0:T(8,128)S(1)} %bitcast.29, f32[16,8,128]{2,1,0:T(8,128)S(1)} %get-tuple-element.49.target_ref, ...), custom_call_target="tpu_custom_call" | custom-call | tf_op jit(solution)/shard_map/cond/branch_1_fun/pallas_call | solution.py:565
  79.3 9.4 %all_to_all.47.part_ref = f32[16,16,128]{2,1,0:T(8,128)S(1)} all-to-all(f32[16,16,128]{2,1,0:T(8,128)S(1)} %bitcast.32), channel_id=1, replica_groups=mesh['blk'=16,'rep'=16] {'blk'}, dimensions={0} | all-to-all | bytes 262144 | tf_op jit(solution)/shard_map/cond/branch_1_fun/all_to_all | solution.py:665
  88.7 13.6 %all_to_all.48 = f32[16,16,128]{2,1,0:T(8,128)S(1)} all-to-all(f32[16,16,128]{2,1,0:T(8,128)S(1)} %branch_1_fun.8), channel_id=1, replica_groups=mesh['blk'=16,'rep'=16] {'rep'}, dimensions={0} | all-to-all | bytes 262144 | tf_op jit(solution)/shard_map/cond/branch_1_fun/all_to_all | solution.py:674
  102.3 1.5 %branch_1_fun.9 = (f32[6,4096]{1,0:T(8,128)}, f32[6,4096]{1,0:T(8,128)}) custom-call(s32[8,128]{1,0:T(8,128)S(1)} %get-tuple-element.43.table_ref, f32[32,8,128]{2,1,0:T(8,128)S(1)} %bitcast.24, f32[6,4096]{1,0:T(8,128)S(1)} %get-tuple-element.55.kin_ref, f32[6,4096]{1,0:T(8,128)S(1)} %get-tuple-element.56.der_ref, f32[1,4096]{1,0:T(1,128)S(1)} %get-tuple-element.57.last_ref), custom_call_target="tpu_custom_call" | custom-call | tf_op jit(solution)/shard_map/cond/branch_1_fun/pallas_call | solution.py:565
  (3 shorter events, 0.0 us)
Async XLA Ops:
  3.0 5.6 %copy-start = (f32[6,4096]{1,0:T(8,128)S(1)}, f32[6,4096]{1,0:T(8,128)}, u32[]{:S(2)}) copy-start(f32[6,4096]{1,0:T(8,128)} %kin_ref.3) | copy-start | bytes 294916
  3.0 5.6 %copy-start.1 = (f32[6,4096]{1,0:T(8,128)S(1)}, f32[6,4096]{1,0:T(8,128)}, u32[]{:S(2)}) copy-start(f32[6,4096]{1,0:T(8,128)} %der_ref.3) | copy-start | bytes 294916
  3.0 5.6 %copy-start.2 = (f32[4096]{0:T(1024)S(1)}, f32[4096]{0:T(1024)}, u32[]{:S(2)}) copy-start(f32[4096]{0:T(1024)} %param.11) | copy-start | bytes 49156
  3.0 5.6 %copy-start.3 = (f32[4096]{0:T(1024)S(1)}, f32[4096]{0:T(1024)}, u32[]{:S(2)}) copy-start(f32[4096]{0:T(1024)} %param.10) | copy-start | bytes 49156
  3.0 13.3 %all-to-all-start.9 = ((f32[16,32,128]{2,1,0:T(8,128)}), f32[16,32,128]{2,1,0:T(8,128)S(1)}, u32[]{:S(2)}, u32[]{:S(2)}) async-start(f32[16,32,128]{2,1,0:T(8,128)} %get-tuple-element.66), calls=%async_computation.9 | async-start | bytes 524288 | tf_op jit(solution)/shard_map/all_to_all | solution.py:696
  8.6 7.7 %copy-start.4 = (s32[2,16,16,2]{2,3,1,0:T(2,128)S(1)}, s32[2,16,16,2]{2,3,1,0:T(2,128)}, u32[]{:S(2)}) copy-start(s32[2,16,16,2]{2,3,1,0:T(2,128)} %param.12) | copy-start | bytes 12292
  8.6 7.7 %copy-start.5 = (s32[2,16,16]{2,1,0:T(8,128)S(1)}, s32[2,16,16]{2,1,0:T(8,128)}, u32[]{:S(2)}) copy-start(s32[2,16,16]{2,1,0:T(8,128)} %count_ref.1) | copy-start | bytes 6148
  31.8 1.3 %collective-permute-start = (f32[96,128]{1,0:T(8,128)S(1)}, f32[96,128]{1,0:T(8,128)S(1)}, u32[]{:S(2)}, u32[]{:S(2)}) collective-permute-start(f32[96,128]{1,0:T(8,128)S(1)} %bitcast.30), channel_id=1, source_target_pairs={{0,16},{16,0},{32,48},{48,32},{64,80},{80,64},{96,112},{112,96},{1... | collective-permute-start | bytes 147464 | tf_op jit(solution)/shard_map/cond/branch_1_fun/ppermute | solution.py:629
  33.1 4.4 %collective-permute-start.1 = (f32[96,128]{1,0:T(8,128)S(1)}, f32[96,128]{1,0:T(8,128)S(1)}, u32[]{:S(2)}, u32[]{:S(2)}) collective-permute-start(f32[96,128]{1,0:T(8,128)S(1)} %bitcast_add_fusion), channel_id=1, source_target_pairs={{0,32},{16,48},{32,0},{48,16},{64,96},{80,112},{96,64},{112,80},{1... | collective-permute-start | bytes 147464 | tf_op jit(solution)/shard_map/cond/branch_1_fun/ppermute | solution.py:629
  37.5 6.2 %collective-permute-start.4 = (f32[96,128]{1,0:T(8,128)S(1)}, f32[96,128]{1,0:T(8,128)S(1)}, u32[]{:S(2)}, u32[]{:S(2)}) collective-permute-start(f32[96,128]{1,0:T(8,128)S(1)} %add.5), channel_id=1, source_target_pairs={{0,128},{16,144},{32,160},{48,176},{64,192},{80,208},{96,224},{112... | collective-permute-start | bytes 147464 | tf_op jit(solution)/shard_map/cond/branch_1_fun/ppermute | solution.py:629
  38.8 5.4 %collective-permute-start.3 = (f32[96,128]{1,0:T(8,128)S(1)}, f32[96,128]{1,0:T(8,128)S(1)}, u32[]{:S(2)}, u32[]{:S(2)}) collective-permute-start(f32[96,128]{1,0:T(8,128)S(1)} %add.5), channel_id=1, source_target_pairs={{0,192},{16,208},{32,224},{48,240},{64,128},{80,144},{96,160},{112... | collective-permute-start | bytes 147464 | tf_op jit(solution)/shard_map/cond/branch_1_fun/ppermute | solution.py:629
  40.3 4.1 %collective-permute-start.2 = (f32[96,128]{1,0:T(8,128)S(1)}, f32[96,128]{1,0:T(8,128)S(1)}, u32[]{:S(2)}, u32[]{:S(2)}) collective-permute-start(f32[96,128]{1,0:T(8,128)S(1)} %add.5), channel_id=1, source_target_pairs={{0,64},{16,80},{32,96},{48,112},{64,0},{80,16},{96,32},{112,48},{1... | collective-permute-start | bytes 147464 | tf_op jit(solution)/shard_map/cond/branch_1_fun/ppermute | solution.py:629
